TPU v7x, 128 devices: a whole 4x4x4 slice. The times are simulated.
128 devices in a mesh: hi: 4 (over z_lo, core), lo: 32 (over x, y, z_hi).
Axes of the slice: x: 4, y: 4, z: 4 (z_hi: 2, z_lo: 2; z = z_hi * 2 + z_lo), core: 2. Of those that a mesh axis runs over, the one named last changes fastest.
Arguments:
- blocks: bfloat16 [8192, 128, 128], P(('hi', 'lo')), may hold values from -6 to 6
- diag_factors: bfloat16 [4, 8192, 128, 128], P(None, ('hi', 'lo')), may hold values from -0.375 to 0.375
- off_factors: bfloat16 [4, 8192, 128, 128], P(None, ('hi', 'lo')), may hold values from -0.375 to 0.375
- partner_maps: int32 [4, 64], replicated, may hold values from 0 to 63, each once within a row
Outputs:
- summed: bfloat16 [2048, 128, 128], P(('lo', 'hi'))
Inputs may be any that keep to these rules, and one draw needn't show every extreme that they name: Each row of partner_maps is a permutation of 0 to 63.
All inputs are finite; a program needn't handle non-finite values.
Results may differ from a plain program's by a relative error of at most 0.009.
Values may be sent and summed in bfloat16 or wider, within the bound.
No kernel may reach another device: no remote copies, remote signals or barrier semaphores. Data moves between devices by JAX's collectives and lax.ppermute only.
A program may use at most 128 MiB of HBM per device.

v0:
```python
import jax
import jax.numpy as jnp
from jax import lax
from jax.sharding import PartitionSpec as P


def partner_2(array, axis, apart):
    return lax.ppermute(array, axis, [(i, i ^ 1 << apart) for i in range(lax.axis_size(axis))])


def apply_factor(factor, data):
    return jnp.einsum("bij,brj->bri", factor, data, preferred_element_type=jnp.float32)


def body(blocks, diag_factors, off_factors, partner_maps):
    current = blocks
    top = lax.axis_size("lo").bit_length() - 1
    for level, bit in enumerate((0, 1, top - 1)):
        partner = partner_2(current, "lo", bit)
        partner = jnp.take(partner, partner_maps[level], axis=0)
        mixed = apply_factor(diag_factors[level], current) + apply_factor(
            off_factors[level], partner
        )
        current = mixed.astype(jnp.bfloat16)
    own = apply_factor(diag_factors[3], current)
    moved = apply_factor(off_factors[3], current)
    moved = partner_2(moved.astype(jnp.bfloat16), "hi", 1).astype(moved.dtype)
    local = own + jnp.take(moved, partner_maps[3], axis=0)
    whole = lax.psum(local, "hi")
    count = local.shape[0] // lax.axis_size("hi")
    share = lax.dynamic_slice_in_dim(whole, lax.axis_index("hi") * count, count, 0)
    return share.astype(jnp.bfloat16)


def solution(mesh):
    in_specs = (
        P(("hi", "lo"), None, None),
        P(None, ("hi", "lo"), None, None),
        P(None, ("hi", "lo"), None, None),
        P(),
    )
    out_specs = P(("lo", "hi"), None, None)
    return jax.shard_map(body, mesh=mesh, in_specs=in_specs, out_specs=out_specs, check_vma=False)
```

profile of v0, /device:TPU:1, one launch (start us, length us, event | category | flops | bytes accessed | tf_op | source)
XLA Modules:
  0.0 308.4 jit_solution(17153876735819277330)
XLA Ops:
  0.0 4.4 %collective-permute-start = (bf16[64,128,128]{2,1,0:T(8,128)(2,1)}, bf16[64,128,128]{2,1,0:T(8,128)(2,1)}, u32[]{:S(2)}, u32[]{:S(2)}) collective-permute-start(bf16[64,128,128]{2,1,0:T(8,128)(2,1)} %param.6), channel_id=1, source_target_pairs={{0,1},{1,0},{2,3},{3,2},{4,5},{5,4},{6,7},{7,6},{8,9},{9,8},{10,11... | collective-permute-start | bytes 6291464 | tf_op jit(solution)/shard_map/ppermute | solution.py:8
  4.4 0.8 compare_and_fusion
  5.3 5.7 %fusion.11 = f32[64,128,128]{2,1,0:T(8,128)} fusion(bf16[64,128,128]{2,1,0:T(8,128)(2,1)} %param.6, bf16[4,64,128,128]{3,2,1,0:T(8,128)(2,1)} %param.7), kind=kOutput, calls=%fused_computation.19 | convolution fusion | flops 268435456 | bytes 8388608 | tf_op jit(solution)/shard_map/bij,brj->bri/dot_general | solution.py:12
  11.0 39.1 %collective-permute-done = bf16[64,128,128]{2,1,0:T(8,128)(2,1)} collective-permute-done((bf16[64,128,128]{2,1,0:T(8,128)(2,1)}, bf16[64,128,128]{2,1,0:T(8,128)(2,1)}, u32[]{:S(2)}, u32[]{:S(2)}) %collective-permute-start) | collective-permute-done | bytes 2097184 | tf_op jit(solution)/shard_map/ppermute | solution.py:8
  50.1 2.5 gather_fusion.1
  52.6 4.4 %add_convert_fusion.2 = bf16[64,128,128]{2,1,0:T(8,128)(2,1)S(1)} fusion(f32[64,128,128]{2,1,0:T(8,128)} %fusion.11, bf16[64,128,128]{2,1,0:T(8,128)(2,1)S(1)} %gather_fusion.1, bf16[4,64,128,128]{3,2,1,0:T(8,128)(2,1)} %param.8, pred[64]{0:T(512)(128)(4,1)S(1)} %get-tuple-element.16), kind=kOutput, calls=%fused_computation.7 | convolution fusion | flops 271581184 | bytes 10485824 | tf_op jit(solution)/shard_map/bij,brj->bri/dot_general | solution.py:12
  57.1 1.4 collective-permute-start.1
  58.5 5.1 %fusion.8 = f32[64,128,128]{2,1,0:T(8,128)} fusion(bf16[64,128,128]{2,1,0:T(8,128)(2,1)S(1)} %add_convert_fusion.2, bf16[4,64,128,128]{3,2,1,0:T(8,128)(2,1)} %param.7), kind=kOutput, calls=%fused_computation.16 | convolution fusion | flops 268435456 | bytes 8388608 | tf_op jit(solution)/shard_map/bij,brj->bri/dot_general | solution.py:12
  63.6 39.6 %collective-permute-done.1 = bf16[64,128,128]{2,1,0:T(8,128)(2,1)} collective-permute-done((bf16[64,128,128]{2,1,0:T(8,128)(2,1)S(1)}, bf16[64,128,128]{2,1,0:T(8,128)(2,1)}, u32[]{:S(2)}, u32[]{:S(2)}) %collective-permute-start.1) | collective-permute-done | bytes 2097184 | tf_op jit(solution)/shard_map/ppermute | solution.py:8
  103.2 2.5 gather_fusion.2
  105.7 4.5 %add_convert_fusion.1 = bf16[64,128,128]{2,1,0:T(8,128)(2,1)S(1)} fusion(f32[64,128,128]{2,1,0:T(8,128)} %fusion.8, bf16[64,128,128]{2,1,0:T(8,128)(2,1)S(1)} %gather_fusion.2, bf16[4,64,128,128]{3,2,1,0:T(8,128)(2,1)} %param.8, pred[64]{0:T(512)(128)(4,1)S(1)} %get-tuple-element.14), kind=kOutput, calls=%fused_computation.6 | convolution fusion | flops 271581184 | bytes 10485824 | tf_op jit(solution)/shard_map/bij,brj->bri/dot_general | solution.py:12
  110.2 2.8 collective-permute-start.2
  113.0 5.1 %fusion.5 = f32[64,128,128]{2,1,0:T(8,128)} fusion(bf16[64,128,128]{2,1,0:T(8,128)(2,1)S(1)} %add_convert_fusion.1, bf16[4,64,128,128]{3,2,1,0:T(8,128)(2,1)} %param.7), kind=kOutput, calls=%fused_computation.13 | convolution fusion | flops 268435456 | bytes 8388608 | tf_op jit(solution)/shard_map/bij,brj->bri/dot_general | solution.py:12
  118.1 38.6 %collective-permute-done.2 = bf16[64,128,128]{2,1,0:T(8,128)(2,1)S(1)} collective-permute-done((bf16[64,128,128]{2,1,0:T(8,128)(2,1)S(1)}, bf16[64,128,128]{2,1,0:T(8,128)(2,1)S(1)}, u32[]{:S(2)}, u32[]{:S(2)}) %collective-permute-start.2) | collective-permute-done | bytes 2097184 | tf_op jit(solution)/shard_map/ppermute | solution.py:8
  156.7 2.1 gather_fusion.3
  158.8 5.1 %add_convert_fusion = bf16[64,128,128]{2,1,0:T(8,128)(2,1)S(1)} fusion(f32[64,128,128]{2,1,0:T(8,128)} %fusion.5, bf16[64,128,128]{2,1,0:T(8,128)(2,1)} %gather_fusion.3, bf16[4,64,128,128]{3,2,1,0:T(8,128)(2,1)} %param.8, pred[64]{0:T(512)(128)(4,1)S(1)} %get-tuple-element.6), kind=kOutput, calls=%fused_computation.5 | convolution fusion | flops 271581184 | bytes 10485824 | tf_op jit(solution)/shard_map/bij,brj->bri/dot_general | solution.py:12
  163.9 4.5 %fusion.27 = bf16[64,128,128]{2,1,0:T(8,128)(2,1)} fusion(bf16[64,128,128]{2,1,0:T(8,128)(2,1)S(1)} %add_convert_fusion, bf16[4,64,128,128]{3,2,1,0:T(8,128)(2,1)} %param.8), kind=kOutput, calls=%fused_computation.35 | convolution fusion | flops 269484032 | bytes 6291456 | tf_op jit(solution)/shard_map/bij,brj->bri/dot_general | solution.py:12
  168.4 0.1 collective-permute-start.3
  168.5 0.7 fusion.33
  169.2 5.1 %fusion.2 = f32[64,128,128]{2,1,0:T(8,128)} fusion(bf16[64,128,128]{2,1,0:T(8,128)(2,1)S(1)} %add_convert_fusion, bf16[4,64,128,128]{3,2,1,0:T(8,128)(2,1)} %param.7), kind=kOutput, calls=%fused_computation.10 | convolution fusion | flops 268435456 | bytes 8388608 | tf_op jit(solution)/shard_map/bij,brj->bri/dot_general | solution.py:12
  174.3 38.5 %collective-permute-done.3 = bf16[64,128,128]{2,1,0:T(8,128)(2,1)} collective-permute-done((bf16[64,128,128]{2,1,0:T(8,128)(2,1)}, bf16[64,128,128]{2,1,0:T(8,128)(2,1)}, u32[]{:S(2)}, u32[]{:S(2)}) %collective-permute-start.3) | collective-permute-done | bytes 2097184 | tf_op jit(solution)/shard_map/ppermute | solution.py:8
  212.8 4.1 %convert_element_type.22 = f32[64,128,128]{2,1,0:T(8,128)} convert(bf16[64,128,128]{2,1,0:T(8,128)(2,1)} %collective-permute-done.3) | non-fusion elementwise | flops 1048576 | bytes 6291456 | tf_op jit(solution)/shard_map/convert_element_type | solution.py:27
  216.9 5.0 %gather_fusion = f32[64,128,128]{2,1,0:T(8,128)} fusion(f32[64,128,128]{2,1,0:T(8,128)} %convert_element_type.22, s32[1024]{0:T(1024)S(1)} %pad_clamp_fusion), kind=kCustom, calls=%fused_computation.3 | custom fusion | bytes 8388864 | tf_op jit(solution)/shard_map/jit(_take)/gather | solution.py:28
  221.8 5.9 %select_add_fusion = f32[64,128,128]{2,1,0:T(8,128)} fusion(f32[64,128,128]{2,1,0:T(8,128)} %fusion.2, f32[64,128,128]{2,1,0:T(8,128)} %gather_fusion, pred[64]{0:T(512)(128)(4,1)S(1)} %get-tuple-element.13), kind=kLoop, calls=%fused_computation.4 | loop fusion | flops 2097152 | bytes 12582976 | tf_op jit(solution)/shard_map/add | solution.py:28
  227.7 79.9 %all-reduce.1 = bf16[64,128,128]{2,1,0:T(8,128)(2,1)S(1)} all-reduce(f32[64,128,128]{2,1,0:T(8,128)} %select_add_fusion), channel_id=1, replica_groups=mesh['hi'=4,'lo'=32] {'hi'}, use_global_device_ids=true, to_apply=%region_0.0 | all-reduce | flops 1048576 | bytes 6291456 | tf_op jit(solution)/shard_map/psum | solution.py:29
  307.6 0.8 dynamic-slice_convert_fusion
  (4 shorter events, 0.0 us)
Async XLA Ops:
  0.0 50.1 %collective-permute-start = (bf16[64,128,128]{2,1,0:T(8,128)(2,1)}, bf16[64,128,128]{2,1,0:T(8,128)(2,1)}, u32[]{:S(2)}, u32[]{:S(2)}) collective-permute-start(bf16[64,128,128]{2,1,0:T(8,128)(2,1)} %param.6), channel_id=1, source_target_pairs={{0,1},{1,0},{2,3},{3,2},{4,5},{5,4},{6,7},{7,6},{8,9},{9,8},{10,11... | collective-permute-start | bytes 6291464 | tf_op jit(solution)/shard_map/ppermute | solution.py:8
  57.1 46.1 %collective-permute-start.1 = (bf16[64,128,128]{2,1,0:T(8,128)(2,1)S(1)}, bf16[64,128,128]{2,1,0:T(8,128)(2,1)}, u32[]{:S(2)}, u32[]{:S(2)}) collective-permute-start(bf16[64,128,128]{2,1,0:T(8,128)(2,1)S(1)} %add_convert_fusion.2), channel_id=1, source_target_pairs={{0,2},{1,3},{2,0},{3,1},{4,6},{5,7},{6,4},{7,5},{8,10},{9,11},{10,... | collective-permute-start | bytes 6291464 | tf_op jit(solution)/shard_map/ppermute | solution.py:8
  110.2 46.5 %collective-permute-start.2 = (bf16[64,128,128]{2,1,0:T(8,128)(2,1)S(1)}, bf16[64,128,128]{2,1,0:T(8,128)(2,1)S(1)}, u32[]{:S(2)}, u32[]{:S(2)}) collective-permute-start(bf16[64,128,128]{2,1,0:T(8,128)(2,1)S(1)} %add_convert_fusion.1), channel_id=1, source_target_pairs={{0,16},{1,17},{2,18},{3,19},{4,20},{5,21},{6,22},{7,23},{8,24},{9,... | collective-permute-start | bytes 6291464 | tf_op jit(solution)/shard_map/ppermute | solution.py:8
  168.4 44.4 %collective-permute-start.3 = (bf16[64,128,128]{2,1,0:T(8,128)(2,1)}, bf16[64,128,128]{2,1,0:T(8,128)(2,1)}, u32[]{:S(2)}, u32[]{:S(2)}) collective-permute-start(bf16[64,128,128]{2,1,0:T(8,128)(2,1)} %fusion.27), channel_id=1, source_target_pairs={{0,64},{32,96},{64,0},{96,32},{1,65},{33,97},{65,1},{97,33},{2,66}... | collective-permute-start | bytes 6291464 | tf_op jit(solution)/shard_map/ppermute | solution.py:8
where the time goes:
time: 309 us; the launch traced here: 308 us
  waiting for transfers between devices  156 us (50%)
  blocking collectives  79.9 us (26%)
  matrix products  39.5 us (13%)
  local copies, waits for them, and re-layouts  13 us (4%)
  other arithmetic  11.5 us (4%)
  starting transfers between devices  8.68 us (3%)
    ppermute x4, waiting for transfers between devices, partner_2(): lax.ppermute(array, axis, [(i, i ^ 1 << apart) for i in range(lax.axis_si...  156 us
    psum x1, blocking collectives, body(): whole = lax.psum(local, 'hi')  79.9 us
    dot_general x8, matrix products, apply_factor(): jnp.einsum('bij,brj->bri', factor, data, preferred_element_type=jnp.float32)  39.5 us
    ppermute x4, starting transfers between devices, partner_2(): lax.ppermute(array, axis, [(i, i ^ 1 << apart) for i in range(lax.axis_si...  8.68 us
    gather x3, local copies, waits for them, and re-layouts, body(): partner = jnp.take(partner, partner_maps[level], axis=0)  7.21 us
  transfers between devices with their start and end apart: 4, of which 4 were waited for; matrix products, arithmetic and copies ran while one was open for 7% of the time, Pallas kernels for 0%

commit v1 on v0

v1 whole, which is shorter than its diff:
```python
import functools

import jax
import jax.numpy as jnp
from jax import lax
from jax.experimental import pallas as pl
from jax.experimental.pallas import tpu as pltpu
from jax.sharding import PartitionSpec as P

BF = jnp.bfloat16
F32 = jnp.float32
VM = pl.BlockSpec(memory_space=pltpu.VMEM)
SM = pl.BlockSpec(memory_space=pltpu.SMEM)
ANY = pl.BlockSpec(memory_space=pl.ANY)
NB = 64
P_ = 128
PIECES = ((0, 64, (21, 22, 21)), (64, 64, (21, 22, 21)))
DEPTH = 2
CYC, NXT, ST, SRC, TJ, POS, PM3 = range(7)


def partner_2(array, axis, apart):
    return lax.ppermute(array, axis, [(i, i ^ 1 << apart) for i in range(lax.axis_size(axis))])


def mm(left, right):
    return lax.dot_general(left, right, (((1,), (1,)), ((), ())), preferred_element_type=F32)


def cat(a, b):
    return jnp.concatenate([a, b], axis=1)


def call(kernel, name, outs, ins, specs, dep, scratch=(), mb=4, out_specs=None, cost=2000000):
    outs = tuple(outs)
    extra = tuple(dep)

    def run(*refs):
        refs = list(refs)
        n = len(ins)
        del refs[n : n + len(extra)]
        kernel(*refs)

    return pl.pallas_call(
        run,
        out_shape=outs,
        in_specs=list(specs) + [ANY] * len(extra),
        out_specs=tuple(out_specs or [VM] * len(outs)),
        scratch_shapes=list(scratch),
        compiler_params=pltpu.CompilerParams(vmem_limit_bytes=mb << 20),
        cost_estimate=pl.CostEstimate(flops=0, bytes_accessed=cost, transcendentals=0),
        name=name,
    )(*ins, *extra)


def bounds(sizes):
    edge = [0]
    for size in sizes:
        edge.append(edge[-1] + size)
    zed = [0] + [e + 1 for e in edge[1:-1]] + [NB]
    return edge, zed


def slots(piece):
    sizes = PIECES[piece][2]
    _, zed = bounds(sizes)
    return max(*sizes, *(b - a for a, b in zip(zed, zed[1:])))


def pad(out, used):
    for i in range(used, out.shape[0]):
        out[i] = jnp.zeros(out.shape[1:], out.dtype)


def gather_z(order, x0, out, piece, k):
    r0, rows, sizes = PIECES[piece]
    _, zed = bounds(sizes)
    for q in range(zed[k], zed[k + 1]):
        out[q - zed[k]] = x0[order[SRC, q], pl.ds(r0, rows), :]
    pad(out, zed[k + 1] - zed[k])


def head_kernel(first, pm_hbm, x_hbm, walk, x0, *rest):
    zouts, (pm, seen, sem) = rest[: len(first)], rest[len(first):]
    maps = pltpu.make_async_copy(pm_hbm, pm, sem.at[0])
    data = pltpu.make_async_copy(x_hbm, x0, sem.at[1])
    maps.start()
    data.start()
    for i in range(NB):
        seen[i] = 0
    maps.wait()

    def step(p, carry):
        cur, start, begin, scan = carry
        walk[CYC, p] = cur
        walk[ST, p] = begin
        seen[cur] = 1
        nxt = pm[1, cur]
        closes = nxt == start
        walk[NXT, p] = jnp.where(closes, begin, p + 1)

        def find():
            return lax.while_loop(
                lambda s: jnp.logical_and(s < NB - 1, seen[s] == 1), lambda s: s + 1, scan
            )

        scan = lax.cond(closes, find, lambda: scan)
        cur = jnp.where(closes, scan, nxt)
        start = jnp.where(closes, scan, start)
        begin = jnp.where(closes, p + 1, begin)
        return cur, start, begin, scan

    zero = jnp.int32(0)
    lax.fori_loop(0, NB, step, (zero, zero, zero, zero))
    data.wait()
    for (piece, k), out in zip(first, zouts):
        r0, rows, sizes = PIECES[piece]
        _, zed = bounds(sizes)
        for q in range(zed[k], zed[k + 1]):
            out[q - zed[k]] = x0[pm[0, walk[CYC, q]], pl.ds(r0, rows), :]
        pad(out, zed[k + 1] - zed[k])


def load_copies(level, d_ref, o_ref, w_ref, sem):
    return [
        pltpu.make_async_copy(ref.at[level], w_ref.at[half], sem.at[half])
        for half, ref in enumerate((d_ref, o_ref))
    ]


def tables_kernel(pm, walk, d_ref, o_ref, order, *refs):
    w_refs, (inv, sem) = refs[:4], refs[4:]
    copies = []
    for level in range(4):
        copies += load_copies(level, d_ref, o_ref, w_refs[level], sem.at[level])
    for copy in copies:
        copy.start()

    def invert(i, _):
        inv[pm[2, i]] = i
        return 0

    lax.fori_loop(0, NB, invert, 0, unroll=8)

    def fill(p, _):
        c = walk[CYC, p]
        order[CYC, p] = c
        order[SRC, p] = pm[0, c]
        order[NXT, p] = walk[NXT, p]
        order[ST, p] = walk[ST, p]
        order[TJ, p] = inv[c]
        order[POS, c] = p
        order[PM3, p] = pm[3, p]
        return 0

    lax.fori_loop(0, NB, fill, 0, unroll=8)
    for copy in copies:
        copy.wait()


def factors(w, j):
    return cat(w[0, j], w[1, j])


def level0_kernel(piece, k, after, *refs):
    refs = list(refs)
    order, x0, zin, w = refs[:4]
    del refs[:4]
    before = refs.pop(0) if k else None
    xs, msg = refs[:2]
    r0, rows, sizes = PIECES[piece]
    edge, zed = bounds(sizes)
    lo, count = edge[k], sizes[k]
    if k:
        xs[0] = before[sizes[k - 1]]
        begin = order[ST, lo]
        xs[count + 1] = before[jnp.where(begin >= edge[k - 1], begin - edge[k - 1], sizes[k - 1] + 1)]
    for q in range(zed[k], zed[k + 1]):
        c = order[CYC, q]
        mixed = mm(cat(x0[c, pl.ds(r0, rows), :], zin[q - zed[k]]), factors(w, c))
        xs[q - lo] = mixed.astype(BF)
    for i in range(count):
        nxt = order[NXT, lo + i]
        msg[i] = xs[jnp.where(nxt >= lo, nxt - lo, count + 1)]
    pad(msg, count)
    if after is not None:
        gather_z(order, x0, refs[2], *after)


def level1_kernel(piece, k, order, xs, yin, w, out):
    _, _, sizes = PIECES[piece]
    edge, _ = bounds(sizes)
    for i in range(sizes[k]):
        mixed = mm(cat(xs[i], yin[i]), factors(w, order[CYC, edge[k] + i]))
        out[i] = mixed.astype(BF)
    pad(out, sizes[k])


def early_kernel(piece, order, w, *refs):
    _, _, sizes = PIECES[piece]
    edge, _ = bounds(sizes)
    n = len(sizes)
    own, got, (x2, x3) = refs[:n], refs[n : 2 * n - 1], refs[2 * n - 1 :]
    for k in range(n):
        for i in range(sizes[k]):
            x2[edge[k] + i] = own[k][i]
    for k in range(n - 1):
        for i in range(sizes[k]):
            j = order[TJ, edge[k] + i]
            x3[edge[k] + i] = mm(cat(x2[order[POS, j]], got[k][i]), factors(w, j)).astype(BF)


def products(order, w3, full, quarter, out, base):
    q = NB // 4
    for i in range(q):
        j = quarter * q + i
        other = order[PM3, j]
        total = mm(cat(full[j], full[other]), cat(w3[0, j], w3[1, other]))
        out[base + i] = total.astype(out.dtype)


def near_far(order, w3, full, send, keep, far, near):
    me = lax.axis_index("hi")
    z, core = me // 2, me % 2
    base = 0
    for chip in ([1 - z] if far else []) + ([z] if near else []):
        products(order, w3, full, 2 * chip + 1 - core, send, base)
        products(order, w3, full, 2 * chip + core, keep, base)
        base += NB // 4


def late_kernel(piece, near, order, w, w3, x2, x3, got, send, keep, full):
    _, _, sizes = PIECES[piece]
    edge, _ = bounds(sizes)
    last = edge[-2]
    for i in range(last):
        full[order[TJ, i]] = x3[i]
    for i in range(sizes[-1]):
        j = order[TJ, last + i]
        full[j] = mm(cat(x2[order[POS, j]], got[i]), factors(w, j)).astype(BF)
    near_far(order, w3, full, send, keep, True, near)


def rest_kernel(order, w3, full, send, keep):
    near_far(order, w3, full, send, keep, False, True)


def join_kernel(keep, got, send, own=None):
    q = NB // 4
    send[...] = (keep[:q] + got[:q].astype(F32)).astype(BF)
    if own is not None:
        own[...] = (keep[q:] + got[q:].astype(F32))


def final_kernel(*refs):
    out = refs[-1]
    for piece, (r0, rows, _) in enumerate(PIECES):
        if piece < len(PIECES) - 1:
            own = refs[2 * piece][...]
            far = refs[2 * piece + 1]
        else:
            own = refs[2 * piece][...] + refs[2 * piece + 1][...].astype(F32)
            far = refs[2 * piece + 2]
        out[:, pl.ds(r0, rows), :] = (own + far[...].astype(F32)).astype(BF)


def plan():
    chunks = [(p, k) for p in range(len(PIECES)) for k in range(len(PIECES[p][2]))]
    count = len(chunks)
    steps = []
    for s in range(count):
        steps.append(("level0", *chunks[s]))
        if s:
            steps.append(("level1", *chunks[s - 1]))
    last = steps.pop()
    steps += [("early", 0, 0), last, ("late", 0, 0), ("level1", *chunks[-1])]
    steps += [("early", 1, 0), ("join", 0, 0), ("late", 1, 0), ("rest", 1, 0), ("join", 1, 0)]
    return chunks, steps


def body(blocks, diag, off, maps):
    hbm = lambda a: pltpu.with_memory_space_constraint(a, pltpu.HBM)
    blocks, diag, off = hbm(blocks), hbm(diag), hbm(off)
    chunks, steps = plan()

    def zshape(piece, k):
        return pltpu.VMEM((slots(piece), PIECES[piece][1], P_), BF)

    first = chunks[: DEPTH + 1]
    walk, x0, *zmsg = call(
        functools.partial(head_kernel, first),
        "head",
        [jax.ShapeDtypeStruct((3, NB), jnp.int32), pltpu.VMEM((NB, P_, P_), BF)]
        + [zshape(*c) for c in first],
        [hbm(maps), blocks],
        [ANY, ANY],
        (),
        scratch=[pltpu.SMEM((4, NB), jnp.int32), pltpu.SMEM((NB,), jnp.int32), pltpu.SemaphoreType.DMA((2,))],
        out_specs=[SM] + [VM] * (1 + len(first)),
    )
    zin = {c: partner_2(m, "lo", 0) for c, m in zip(first, zmsg)}
    wshape = pltpu.VMEM((2, NB, P_, P_), BF)
    order, *w = call(
        tables_kernel,
        "tables",
        [jax.ShapeDtypeStruct((8, NB), jnp.int32)] + [wshape] * 4,
        [maps, walk, diag, off],
        [SM, SM, ANY, ANY],
        (x0,),
        scratch=[pltpu.SMEM((NB,), jnp.int32), pltpu.SemaphoreType.DMA((4, 2))],
        out_specs=[SM] + [VM] * 4,
    )
    dep = x0
    top = lax.axis_size("lo").bit_length() - 1
    xs, yin, x2, xin, early, late, core, chip = {}, {}, {}, {}, {}, {}, {}, {}
    for kind, piece, k in steps:
        _, rows, sizes = PIECES[piece]
        c = (piece, k)
        name = f"{kind}_{piece}_{k}"
        dep = (dep, *w)
        part = lambda count, dtype: pltpu.VMEM((count, rows, P_), dtype)
        if kind == "level0":
            s = chunks.index(c)
            after = chunks[s + DEPTH] if 0 < s < len(chunks) - DEPTH else None
            outs = [part(sizes[k] + 2, BF), part(slots(piece), BF)]
            outs += [zshape(*after)] if after else []
            ins = [order, x0, zin[c], w[0]] + ([xs[piece, k - 1]] if k else [])
            specs = [SM] + [VM] * (len(ins) - 1)
            xs[c], msg, *more = call(
                functools.partial(level0_kernel, piece, k, after),
                name, outs, ins, specs, dep,
            )
            yin[c] = partner_2(msg, "lo", 1)
            if after:
                zin[after] = partner_2(more[0], "lo", 0)
            dep = xs[c]
        elif kind == "level1":
            s = chunks.index(c) - 2
            if s >= 0:
                dep = (*dep, xin[chunks[s]])
            (x2[c],) = call(
                functools.partial(level1_kernel, piece, k),
                name, [part(slots(piece), BF)],
                [order, xs[c], yin[c], w[1]], [SM, VM, VM, VM], dep,
            )
            xin[c] = partner_2(x2[c], "lo", top - 1)
            dep = x2[c]
        elif kind == "early":
            n = len(sizes)
            ins = [order, w[2]] + [x2[piece, i] for i in range(n)] + [xin[piece, i] for i in range(n - 1)]
            early[piece] = call(
                functools.partial(early_kernel, piece),
                name, [part(NB, BF), part(NB - sizes[-1], BF)],
                ins, [SM] + [VM] * (len(ins) - 1), dep, cost=20000000 if piece else 2000000,
            )
            dep = early[piece][0]
        elif kind == "late":
            split = piece == len(PIECES) - 1
            count = NB // 4 if split else NB // 2
            send, keep, full = call(
                functools.partial(late_kernel, piece, not split),
                name, [part(count, BF), part(count, F32), part(NB, BF)],
                [order, w[2], w[3], *early[piece], xin[piece, len(sizes) - 1]], [SM] + [VM] * 5, dep,
            )
            late[piece] = full
            core[piece] = keep, partner_2(send, "hi", 0)
            dep = keep
        elif kind == "rest":
            if piece:
                dep = (*dep, chip[piece - 1][1])
            send, keep = call(
                rest_kernel,
                name, [part(NB // 4, BF), part(NB // 4, F32)],
                [order, w[3], late[piece]], [SM, VM, VM], dep,
            )
            chip[piece] = keep, partner_2(send, "hi", 0)
            dep = keep
        else:
            split = piece == len(PIECES) - 1
            outs = [part(NB // 4, BF)] + ([] if split else [part(NB // 4, F32)])
            send, *own = call(join_kernel, name, outs, [*core[piece]], [VM, VM], dep)
            chip[piece] = *(chip[piece] if split else own), partner_2(send, "hi", 1)
            dep = send
    ins = [a for piece in range(len(PIECES)) for a in chip[piece]]
    (out,) = call(
        final_kernel, "final", [jax.ShapeDtypeStruct((NB // 4, P_, P_), BF)],
        ins, [VM] * len(ins), (),
    )
    return out


def solution(mesh):
    in_specs = (
        P(("hi", "lo"), None, None),
        P(None, ("hi", "lo"), None, None),
        P(None, ("hi", "lo"), None, None),
        P(),
    )
    out_specs = P(("lo", "hi"), None, None)
    return jax.shard_map(body, mesh=mesh, in_specs=in_specs, out_specs=out_specs, check_vma=False)
```

time: 309 us -> 103 us (0.33)
  waiting for transfers between devices: 156 us -> 22.5 us
  blocking collectives: 79.9 us -> 0 us
  matrix products: 39.5 us -> 0 us
  Pallas kernels: 0 us -> 36.8 us
  starting transfers between devices: 8.68 us -> 42.6 us
  local copies, waits for them, and re-layouts: 13 us -> 0.68 us
  other arithmetic: 11.5 us -> 0 us
    ppermute x4 -> x23, waiting for transfers between devices: 156 us -> 22.5 us  [partner_2(): lax.ppermute(array, axis, [(i, i ^ 1 << apart) for i in range(lax.axis_si...]
    psum x1 -> x0, blocking collectives: 79.9 us -> none  [body(): whole = lax.psum(local, 'hi')]
    dot_general x8 -> x0, matrix products: 39.5 us -> none  [apply_factor(): jnp.einsum('bij,brj->bri', factor, data, preferred_element_type=jnp.float32)]
    pallas_call x0 -> x22, Pallas kernels: none -> 36.8 us  [call(): pl.pallas_call(run, out_shape=outs, in_specs=list(specs) + [ANY] * len(ex...]
    ppermute x4 -> x23, starting transfers between devices: 8.68 us -> 42.6 us  [partner_2(): lax.ppermute(array, axis, [(i, i ^ 1 << apart) for i in range(lax.axis_si...]
    gather x4 -> x0, local copies, waits for them, and re-layouts: 12.2 us -> none  [the longest x3 7.21 us: body(): partner = jnp.take(partner, partner_maps[level], axis=0)]
    add x1 -> x0, other arithmetic: 5.87 us -> none  [body(): local = own + jnp.take(moved, partner_maps[3], axis=0)]
    convert_element_type x1 -> x0, other arithmetic: 4.07 us -> none  [body(): moved = partner_2(moved.astype(jnp.bfloat16), 'hi', 1).astype(moved.dtype)]
  transfers between devices with their start and end apart: 4 -> 23, of which waited for: 4 -> 6; matrix products, arithmetic and copies ran while one was open for 7% -> 0% of each run, Pallas kernels for 0% -> 32%
where the time goes in v1:
time: 103 us
  starting transfers between devices  42.6 us (41%)
  Pallas kernels  36.8 us (36%)
  waiting for transfers between devices  22.5 us (22%)
    ppermute x23, starting transfers between devices, partner_2(): lax.ppermute(array, axis, [(i, i ^ 1 << apart) for i in range(lax.axis_si...  42.6 us
    pallas_call x22, Pallas kernels, call(): pl.pallas_call(run, out_shape=outs, in_specs=list(specs) + [ANY] * len(ex...  36.8 us
    ppermute x23, waiting for transfers between devices, partner_2(): lax.ppermute(array, axis, [(i, i ^ 1 << apart) for i in range(lax.axis_si...  22.5 us
  transfers between devices with their start and end apart: 23, of which 6 were waited for; matrix products, arithmetic and copies ran while one was open for 0% of the time, Pallas kernels for 32%

profile of v1, /device:TPU:1, one launch (start us, length us, event | category | flops | bytes accessed | tf_op | source)
XLA Modules:
  0.0 102.8 jit_solution(2905904514458208034)
XLA Ops:
  0.0 3.3 %head.1 = (s32[3,64]{1,0:T(4,128)S(1)}, bf16[64,128,128]{2,1,0:T(8,128)(2,1)S(1)}, bf16[22,64,128]{2,1,0:T(8,128)(2,1)S(1)}, bf16[22,64,128]{2,1,0:T(8,128)(2,1)S(1)}, bf16[22,64,128]{2,1,0:T(8,128)(2,1)S(1)}) custom-call(s32[4,64]{1,0:T(4,128)} %refs_0_.3, bf16[64,128,128]{2,1,0:T(8,128)(2,1)} %refs_1_.1), custom_call_target="tpu_custom_call" | custom-call | bytes 2000000 | tf_op jit(solution)/shard_map/head/pallas_call | solution.py:44
  3.3 4.5 %collective-permute-start = (bf16[22,64,128]{2,1,0:T(8,128)(2,1)S(1)}, bf16[22,64,128]{2,1,0:T(8,128)(2,1)S(1)}, u32[]{:S(2)}, u32[]{:S(2)}) collective-permute-start(bf16[22,64,128]{2,1,0:T(8,128)(2,1)S(1)} %get-tuple-element.48), channel_id=1, source_target_pairs={{0,1},{1,0},{2,3},{3,2},{4,5},{5,4},{6,7},{7,6},{8,9},{9,8},{10,11... | collective-permute-start | bytes 1081352 | tf_op jit(solution)/shard_map/ppermute | solution.py:23
  8.6 7.2 %tables.1 = (s32[8,64]{1,0:T(8,128)S(1)}, bf16[2,64,128,128]{3,2,1,0:T(8,128)(2,1)S(1)}, bf16[2,64,128,128]{3,2,1,0:T(8,128)(2,1)S(1)}, bf16[2,64,128,128]{3,2,1...) custom-call(s32[4,64]{1,0:T(4,128)S(1)} %copy-done, s32[3,64]{1,0:T(4,128)S(1)} %get-tuple-element.43.refs_1_, ...), custom_call_target="tpu_custom_call" | custom-call | bytes 2000000 | tf_op jit(solution)/shard_map/tables/pallas_call | solution.py:44
  15.9 1.3 %level0_0_0.1 = (bf16[23,64,128]{2,1,0:T(8,128)(2,1)S(1)}, bf16[22,64,128]{2,1,0:T(8,128)(2,1)S(1)}) custom-call(s32[8,64]{1,0:T(8,128)S(1)} %get-tuple-element.45.refs_0_, bf16[64,128,128]{2,1,0:T(8,128)(2,1)S(1)} %get-tuple-element.44.refs_4_.refs_1_, bf16[22,64,128]{2,1,0:T(8,128)(2,1)S(1)} %collective-permute-done.refs_2_, ...), custom_call_target="tpu_custom_call" | custom-call | bytes 2000000 | tf_op jit(solution)/shard_map/level0_0_0/pallas_call | solution.py:44
  17.2 1.4 %collective-permute-start.1 = (bf16[22,64,128]{2,1,0:T(8,128)(2,1)S(1)}, bf16[22,64,128]{2,1,0:T(8,128)(2,1)S(1)}, u32[]{:S(2)}, u32[]{:S(2)}) collective-permute-start(bf16[22,64,128]{2,1,0:T(8,128)(2,1)S(1)} %get-tuple-element.52), channel_id=1, source_target_pairs={{0,2},{1,3},{2,0},{3,1},{4,6},{5,7},{6,4},{7,5},{8,10},{9,11},{10,... | collective-permute-start | bytes 1081352 | tf_op jit(solution)/shard_map/ppermute | solution.py:23
  18.6 2.7 %collective-permute-start.4 = (bf16[22,64,128]{2,1,0:T(8,128)(2,1)S(1)}, bf16[22,64,128]{2,1,0:T(8,128)(2,1)S(1)}, u32[]{:S(2)}, u32[]{:S(2)}) collective-permute-start(bf16[22,64,128]{2,1,0:T(8,128)(2,1)S(1)} %get-tuple-element.56), channel_id=1, source_target_pairs={{0,1},{1,0},{2,3},{3,2},{4,5},{5,4},{6,7},{7,6},{8,9},{9,8},{10,11... | collective-permute-start | bytes 1081352 | tf_op jit(solution)/shard_map/ppermute | solution.py:23
  21.3 2.4 %collective-permute-done.2.refs_2_ = bf16[22,64,128]{2,1,0:T(8,128)(2,1)S(1)} collective-permute-done((bf16[22,64,128]{2,1,0:T(8,128)(2,1)S(1)}, bf16[22,64,128]{2,1,0:T(8,128)(2,1)S(1)}, u32[]{:S(2)}, u32[]{:S(2)}) %collective-permute-start.2) | collective-permute-done | bytes 360480 | tf_op jit(solution)/shard_map/ppermute | solution.py:23
  23.6 1.2 %level0_0_1.1 = (bf16[24,64,128]{2,1,0:T(8,128)(2,1)S(1)}, bf16[22,64,128]{2,1,0:T(8,128)(2,1)S(1)}, bf16[22,64,128]{2,1,0:T(8,128)(2,1)S(1)}) custom-call(s32[8,64]{1,0:T(8,128)S(1)} %get-tuple-element.45.refs_0_, bf16[64,128,128]{2,1,0:T(8,128)(2,1)S(1)} %get-tuple-element.44.refs_4_.refs_1_, bf16[22,64,128]{2,1,0:T(8,128)(2,1)S(1)} %collective-permute-done.2.refs_2_, ...), custom_call_target="tpu_custom_call" | custom-call | bytes 2000000 | tf_op jit(solution)/shard_map/level0_0_1/pallas_call | solution.py:44
  24.9 1.4 %collective-permute-start.3 = (bf16[22,64,128]{2,1,0:T(8,128)(2,1)S(1)}, bf16[22,64,128]{2,1,0:T(8,128)(2,1)S(1)}, u32[]{:S(2)}, u32[]{:S(2)}) collective-permute-start(bf16[22,64,128]{2,1,0:T(8,128)(2,1)S(1)} %get-tuple-element.55), channel_id=1, source_target_pairs={{0,2},{1,3},{2,0},{3,1},{4,6},{5,7},{6,4},{7,5},{8,10},{9,11},{10,... | collective-permute-start | bytes 1081352 | tf_op jit(solution)/shard_map/ppermute | solution.py:23
  26.3 2.6 %collective-permute-start.6 = (bf16[22,64,128]{2,1,0:T(8,128)(2,1)S(1)}, bf16[22,64,128]{2,1,0:T(8,128)(2,1)S(1)}, u32[]{:S(2)}, u32[]{:S(2)}) collective-permute-start(bf16[22,64,128]{2,1,0:T(8,128)(2,1)S(1)} %get-tuple-element.59), channel_id=1, source_target_pairs={{0,1},{1,0},{2,3},{3,2},{4,5},{5,4},{6,7},{7,6},{8,9},{9,8},{10,11... | collective-permute-start | bytes 1081352 | tf_op jit(solution)/shard_map/ppermute | solution.py:23
  28.9 1.2 %level1_0_0.1.refs_5_.refs_2_ = bf16[22,64,128]{2,1,0:T(8,128)(2,1)S(1)} custom-call(s32[8,64]{1,0:T(8,128)S(1)} %get-tuple-element.45.refs_0_, bf16[23,64,128]{2,1,0:T(8,128)(2,1)S(1)} %get-tuple-element.51.refs_4_.refs_5_.refs_1_, bf16[22,64,128]{2,1,0:T(8,128)(2,1)S(1)} %collective-permute-done.1.refs_2_, ...), custom_call_target="tpu_custom_call" | custom-call | bytes 2000000 | tf_op jit(solution)/shard_map/level1_0_0/pallas_call | solution.py:44
  32.2 1.7 %collective-permute-start.5 = (bf16[22,64,128]{2,1,0:T(8,128)(2,1)S(1)}, bf16[22,64,128]{2,1,0:T(8,128)(2,1)S(1)}, u32[]{:S(2)}, u32[]{:S(2)}) collective-permute-start(bf16[22,64,128]{2,1,0:T(8,128)(2,1)S(1)} %get-tuple-element.58), channel_id=1, source_target_pairs={{0,2},{1,3},{2,0},{3,1},{4,6},{5,7},{6,4},{7,5},{8,10},{9,11},{10,... | collective-permute-start | bytes 1081352 | tf_op jit(solution)/shard_map/ppermute | solution.py:23
  34.0 2.7 %collective-permute-start.7 = (bf16[22,64,128]{2,1,0:T(8,128)(2,1)S(1)}, bf16[22,64,128]{2,1,0:T(8,128)(2,1)S(1)}, u32[]{:S(2)}, u32[]{:S(2)}) collective-permute-start(bf16[22,64,128]{2,1,0:T(8,128)(2,1)S(1)} %level1_0_0.1.refs_5_.refs_2_), channel_id=1, source_target_pairs={{0,16},{1,17},{2,18},{3,19},{4,20},{5,21},{6,22},{7,23},{8,24},{9,... | collective-permute-start | bytes 1081352 | tf_op jit(solution)/shard_map/ppermute | solution.py:23
  36.7 2.7 %collective-permute-start.10 = (bf16[22,64,128]{2,1,0:T(8,128)(2,1)S(1)}, bf16[22,64,128]{2,1,0:T(8,128)(2,1)S(1)}, u32[]{:S(2)}, u32[]{:S(2)}) collective-permute-start(bf16[22,64,128]{2,1,0:T(8,128)(2,1)S(1)} %get-tuple-element.62), channel_id=1, source_target_pairs={{0,1},{1,0},{2,3},{3,2},{4,5},{5,4},{6,7},{7,6},{8,9},{9,8},{10,11... | collective-permute-start | bytes 1081352 | tf_op jit(solution)/shard_map/ppermute | solution.py:23
  39.4 1.2 %level1_0_1.1.refs_4_.refs_3_ = bf16[22,64,128]{2,1,0:T(8,128)(2,1)S(1)} custom-call(s32[8,64]{1,0:T(8,128)S(1)} %get-tuple-element.45.refs_0_, bf16[24,64,128]{2,1,0:T(8,128)(2,1)S(1)} %get-tuple-element.54.refs_4_.refs_1_, bf16[22,64,128]{2,1,0:T(8,128)(2,1)S(1)} %collective-permute-done.3.refs_2_, ...), custom_call_target="tpu_custom_call" | custom-call | bytes 2000000 | tf_op jit(solution)/shard_map/level1_0_1/pallas_call | solution.py:44
  40.6 1.3 %level0_1_0.1 = (bf16[23,64,128]{2,1,0:T(8,128)(2,1)S(1)}, bf16[22,64,128]{2,1,0:T(8,128)(2,1)S(1)}, bf16[22,64,128]{2,1,0:T(8,128)(2,1)S(1)}) custom-call(s32[8,64]{1,0:T(8,128)S(1)} %get-tuple-element.45.refs_0_, bf16[64,128,128]{2,1,0:T(8,128)(2,1)S(1)} %get-tuple-element.44.refs_4_.refs_1_, bf16[22,64,128]{2,1,0:T(8,128)(2,1)S(1)} %collective-permute-done.6.refs_2_, ...), custom_call_target="tpu_custom_call" | custom-call | bytes 2000000 | tf_op jit(solution)/shard_map/level0_1_0/pallas_call | solution.py:44
  42.0 2.5 %collective-permute-start.8 = (bf16[22,64,128]{2,1,0:T(8,128)(2,1)S(1)}, bf16[22,64,128]{2,1,0:T(8,128)(2,1)S(1)}, u32[]{:S(2)}, u32[]{:S(2)}) collective-permute-start(bf16[22,64,128]{2,1,0:T(8,128)(2,1)S(1)} %level1_0_1.1.refs_4_.refs_3_), channel_id=1, source_target_pairs={{0,16},{1,17},{2,18},{3,19},{4,20},{5,21},{6,22},{7,23},{8,24},{9,... | collective-permute-start | bytes 1081352 | tf_op jit(solution)/shard_map/ppermute | solution.py:23
  44.5 2.6 %collective-permute-start.9 = (bf16[22,64,128]{2,1,0:T(8,128)(2,1)S(1)}, bf16[22,64,128]{2,1,0:T(8,128)(2,1)S(1)}, u32[]{:S(2)}, u32[]{:S(2)}) collective-permute-start(bf16[22,64,128]{2,1,0:T(8,128)(2,1)S(1)} %get-tuple-element.61), channel_id=1, source_target_pairs={{0,1},{1,0},{2,3},{3,2},{4,5},{5,4},{6,7},{7,6},{8,9},{9,8},{10,11... | collective-permute-start | bytes 1081352 | tf_op jit(solution)/shard_map/ppermute | solution.py:23
  48.3 1.2 %level0_1_1.1 = (bf16[24,64,128]{2,1,0:T(8,128)(2,1)S(1)}, bf16[22,64,128]{2,1,0:T(8,128)(2,1)S(1)}) custom-call(s32[8,64]{1,0:T(8,128)S(1)} %get-tuple-element.45.refs_0_, bf16[64,128,128]{2,1,0:T(8,128)(2,1)S(1)} %get-tuple-element.44.refs_4_.refs_1_, bf16[22,64,128]{2,1,0:T(8,128)(2,1)S(1)} %collective-permute-done.10.refs_2_, ...), custom_call_target="tpu_custom_call" | custom-call | bytes 2000000 | tf_op jit(solution)/shard_map/level0_1_1/pallas_call | solution.py:44
  49.8 2.4 %collective-permute-start.12 = (bf16[22,64,128]{2,1,0:T(8,128)(2,1)S(1)}, bf16[22,64,128]{2,1,0:T(8,128)(2,1)S(1)}, u32[]{:S(2)}, u32[]{:S(2)}) collective-permute-start(bf16[22,64,128]{2,1,0:T(8,128)(2,1)S(1)} %level1_0_2.1.refs_5_.refs_4_), channel_id=1, source_target_pairs={{0,16},{1,17},{2,18},{3,19},{4,20},{5,21},{6,22},{7,23},{8,24},{9,... | collective-permute-start | bytes 1081352 | tf_op jit(solution)/shard_map/ppermute | solution.py:23
  54.8 4.0 %collective-permute-start.16 = (bf16[22,64,128]{2,1,0:T(8,128)(2,1)S(1)}, bf16[22,64,128]{2,1,0:T(8,128)(2,1)S(1)}, u32[]{:S(2)}, u32[]{:S(2)}) collective-permute-start(bf16[22,64,128]{2,1,0:T(8,128)(2,1)S(1)} %level1_1_0.1.refs_5_.refs_2_), channel_id=1, source_target_pairs={{0,16},{1,17},{2,18},{3,19},{4,20},{5,21},{6,22},{7,23},{8,24},{9,... | collective-permute-start | bytes 1081352 | tf_op jit(solution)/shard_map/ppermute | solution.py:23
  58.8 1.8 %early_0_0.1 = (bf16[64,64,128]{2,1,0:T(8,128)(2,1)S(1)}, bf16[43,64,128]{2,1,0:T(8,128)(2,1)S(1)}) custom-call(s32[8,64]{1,0:T(8,128)S(1)} %get-tuple-element.45.refs_0_, bf16[2,64,128,128]{3,2,1,0:T(8,128)(2,1)S(1)} %get-tuple-element.46.refs_7_.refs_8_.refs_1_.refs_10_.refs_9_.refs_5_.refs_6_, bf16[22,64,128]{2,1,0:T(8,128)(2,1)S(1)} %level1_0_0.1.refs_5_.refs_2_, ...), custom_call_target="tpu_custom_call" | custom-call | bytes 2000000 | tf_op jit(solution)/shard_map/early_0_0/pallas_call | solution.py:44
  60.6 1.2 %level1_1_1.1.refs_6_.refs_3_ = bf16[22,64,128]{2,1,0:T(8,128)(2,1)S(1)} custom-call(s32[8,64]{1,0:T(8,128)S(1)} %get-tuple-element.45.refs_0_, bf16[24,64,128]{2,1,0:T(8,128)(2,1)S(1)} %get-tuple-element.63.refs_4_.refs_1_, bf16[22,64,128]{2,1,0:T(8,128)(2,1)S(1)} %collective-permute-done.13.refs_2_, ...), custom_call_target="tpu_custom_call" | custom-call | bytes 2000000 | tf_op jit(solution)/shard_map/level1_1_1/pallas_call | solution.py:44
  61.8 3.6 %late_0_0.1 = (bf16[32,64,128]{2,1,0:T(8,128)(2,1)S(1)}, f32[32,64,128]{2,1,0:T(8,128)S(1)}, bf16[64,64,128]{2,1,0:T(8,128)(2,1)}) custom-call(s32[8,64]{1,0:T(8,128)S(1)} %get-tuple-element.45.refs_0_, bf16[2,64,128,128]{3,2,1,0:T(8,128)(2,1)S(1)} %get-tuple-element.46.refs_7_.refs_8_.refs_1_.refs_10_.refs_9_.refs_5_.refs_6_, ...), custom_call_target="tpu_custom_call" | custom-call | bytes 2000000 | tf_op jit(solution)/shard_map/late_0_0/pallas_call | solution.py:44
  65.4 4.7 %collective-permute-start.14 = (bf16[32,64,128]{2,1,0:T(8,128)(2,1)S(1)}, bf16[32,64,128]{2,1,0:T(8,128)(2,1)S(1)}, u32[]{:S(2)}, u32[]{:S(2)}) collective-permute-start(bf16[32,64,128]{2,1,0:T(8,128)(2,1)S(1)} %get-tuple-element.70), channel_id=1, source_target_pairs={{0,32},{32,0},{64,96},{96,64},{1,33},{33,1},{65,97},{97,65},{2,34}... | collective-permute-start | bytes 1572872 | tf_op jit(solution)/shard_map/ppermute | solution.py:23
  71.6 3.0 %collective-permute-start.19 = (bf16[22,64,128]{2,1,0:T(8,128)(2,1)S(1)}, bf16[22,64,128]{2,1,0:T(8,128)(2,1)S(1)}, u32[]{:S(2)}, u32[]{:S(2)}) collective-permute-start(bf16[22,64,128]{2,1,0:T(8,128)(2,1)S(1)} %level1_1_2.1.refs_4_.refs_7_), channel_id=1, source_target_pairs={{0,16},{1,17},{2,18},{3,19},{4,20},{5,21},{6,22},{7,23},{8,24},{9,... | collective-permute-start | bytes 1081352 | tf_op jit(solution)/shard_map/ppermute | solution.py:23
  74.5 7.1 %collective-permute-done.17.refs_6_ = bf16[22,64,128]{2,1,0:T(8,128)(2,1)S(1)} collective-permute-done((bf16[22,64,128]{2,1,0:T(8,128)(2,1)S(1)}, bf16[22,64,128]{2,1,0:T(8,128)(2,1)S(1)}, u32[]{:S(2)}, u32[]{:S(2)}) %collective-permute-start.17) | collective-permute-done | bytes 360480 | tf_op jit(solution)/shard_map/ppermute | solution.py:23
  81.7 1.7 %early_1_0.1 = (bf16[64,64,128]{2,1,0:T(8,128)(2,1)S(1)}, bf16[43,64,128]{2,1,0:T(8,128)(2,1)S(1)}) custom-call(s32[8,64]{1,0:T(8,128)S(1)} %get-tuple-element.45.refs_0_, bf16[2,64,128,128]{3,2,1,0:T(8,128)(2,1)S(1)} %get-tuple-element.46.refs_7_.refs_8_.refs_1_.refs_10_.refs_9_.refs_5_.refs_6_, bf16[22,64,128]{2,1,0:T(8,128)(2,1)S(1)} %level1_1_0.1.refs_5_.refs_2_, ...), custom_call_target="tpu_custom_call" | custom-call | bytes 20000000 | tf_op jit(solution)/shard_map/early_1_0/pallas_call | solution.py:44
  84.4 5.0 %collective-permute-done.19.refs_5_ = bf16[22,64,128]{2,1,0:T(8,128)(2,1)S(1)} collective-permute-done((bf16[22,64,128]{2,1,0:T(8,128)(2,1)S(1)}, bf16[22,64,128]{2,1,0:T(8,128)(2,1)S(1)}, u32[]{:S(2)}, u32[]{:S(2)}) %collective-permute-start.19) | collective-permute-done | bytes 360480 | tf_op jit(solution)/shard_map/ppermute | solution.py:23
  89.4 2.1 %late_1_0.1 = (bf16[16,64,128]{2,1,0:T(8,128)(2,1)S(1)}, f32[16,64,128]{2,1,0:T(8,128)S(1)}, bf16[64,64,128]{2,1,0:T(8,128)(2,1)S(1)}) custom-call(s32[8,64]{1,0:T(8,128)S(1)} %get-tuple-element.45.refs_0_, bf16[2,64,128,128]{3,2,1,0:T(8,128)(2,1)S(1)} %get-tuple-element.46.refs_7_.refs_8_.refs_1_.refs_10_.refs_9_.refs_5_.refs_6_, ...), custom_call_target="tpu_custom_call" | custom-call | bytes 2000000 | tf_op jit(solution)/shard_map/late_1_0/pallas_call | solution.py:44
  92.3 1.5 %rest_1_0.1 = (bf16[16,64,128]{2,1,0:T(8,128)(2,1)S(1)}, f32[16,64,128]{2,1,0:T(8,128)S(1)}) custom-call(s32[8,64]{1,0:T(8,128)S(1)} %get-tuple-element.45.refs_0_, bf16[2,64,128,128]{3,2,1,0:T(8,128)(2,1)S(1)} %get-tuple-element.47.refs_8_.refs_9_.refs_11_.refs_2_.refs_10_.refs_6_.refs_1_.refs_7_, bf16[64,64,128]{2,1,0:T(8,128)(2,1)S(1)} %get-tuple-element.76.refs_2_, ...), custom_call_target="tpu_custom_call" | custom-call | bytes 2000000 | tf_op jit(solution)/shard_map/rest_1_0/pallas_call | solution.py:44
  95.0 6.8 %collective-permute-done.22.refs_4_ = bf16[16,64,128]{2,1,0:T(8,128)(2,1)S(1)} collective-permute-done((bf16[16,64,128]{2,1,0:T(8,128)(2,1)S(1)}, bf16[16,64,128]{2,1,0:T(8,128)(2,1)S(1)}, u32[]{:S(2)}, u32[]{:S(2)}) %collective-permute-start.22) | collective-permute-done | bytes 262176 | tf_op jit(solution)/shard_map/ppermute | solution.py:23
  (38 shorter events, 12.6 us)
Async XLA Ops:
  3.3 12.6 %collective-permute-start = (bf16[22,64,128]{2,1,0:T(8,128)(2,1)S(1)}, bf16[22,64,128]{2,1,0:T(8,128)(2,1)S(1)}, u32[]{:S(2)}, u32[]{:S(2)}) collective-permute-start(bf16[22,64,128]{2,1,0:T(8,128)(2,1)S(1)} %get-tuple-element.48), channel_id=1, source_target_pairs={{0,1},{1,0},{2,3},{3,2},{4,5},{5,4},{6,7},{7,6},{8,9},{9,8},{10,11... | collective-permute-start | bytes 1081352 | tf_op jit(solution)/shard_map/ppermute | solution.py:23
  7.8 15.9 %collective-permute-start.2 = (bf16[22,64,128]{2,1,0:T(8,128)(2,1)S(1)}, bf16[22,64,128]{2,1,0:T(8,128)(2,1)S(1)}, u32[]{:S(2)}, u32[]{:S(2)}) collective-permute-start(bf16[22,64,128]{2,1,0:T(8,128)(2,1)S(1)} %get-tuple-element.53), channel_id=1, source_target_pairs={{0,1},{1,0},{2,3},{3,2},{4,5},{5,4},{6,7},{7,6},{8,9},{9,8},{10,11... | collective-permute-start | bytes 1081352 | tf_op jit(solution)/shard_map/ppermute | solution.py:23
  7.9 0.7 copy-start
  17.2 11.7 %collective-permute-start.1 = (bf16[22,64,128]{2,1,0:T(8,128)(2,1)S(1)}, bf16[22,64,128]{2,1,0:T(8,128)(2,1)S(1)}, u32[]{:S(2)}, u32[]{:S(2)}) collective-permute-start(bf16[22,64,128]{2,1,0:T(8,128)(2,1)S(1)} %get-tuple-element.52), channel_id=1, source_target_pairs={{0,2},{1,3},{2,0},{3,1},{4,6},{5,7},{6,4},{7,5},{8,10},{9,11},{10,... | collective-permute-start | bytes 1081352 | tf_op jit(solution)/shard_map/ppermute | solution.py:23
  18.6 12.4 %collective-permute-start.4 = (bf16[22,64,128]{2,1,0:T(8,128)(2,1)S(1)}, bf16[22,64,128]{2,1,0:T(8,128)(2,1)S(1)}, u32[]{:S(2)}, u32[]{:S(2)}) collective-permute-start(bf16[22,64,128]{2,1,0:T(8,128)(2,1)S(1)} %get-tuple-element.56), channel_id=1, source_target_pairs={{0,1},{1,0},{2,3},{3,2},{4,5},{5,4},{6,7},{7,6},{8,9},{9,8},{10,11... | collective-permute-start | bytes 1081352 | tf_op jit(solution)/shard_map/ppermute | solution.py:23
  24.9 14.5 %collective-permute-start.3 = (bf16[22,64,128]{2,1,0:T(8,128)(2,1)S(1)}, bf16[22,64,128]{2,1,0:T(8,128)(2,1)S(1)}, u32[]{:S(2)}, u32[]{:S(2)}) collective-permute-start(bf16[22,64,128]{2,1,0:T(8,128)(2,1)S(1)} %get-tuple-element.55), channel_id=1, source_target_pairs={{0,2},{1,3},{2,0},{3,1},{4,6},{5,7},{6,4},{7,5},{8,10},{9,11},{10,... | collective-permute-start | bytes 1081352 | tf_op jit(solution)/shard_map/ppermute | solution.py:23
  26.3 14.3 %collective-permute-start.6 = (bf16[22,64,128]{2,1,0:T(8,128)(2,1)S(1)}, bf16[22,64,128]{2,1,0:T(8,128)(2,1)S(1)}, u32[]{:S(2)}, u32[]{:S(2)}) collective-permute-start(bf16[22,64,128]{2,1,0:T(8,128)(2,1)S(1)} %get-tuple-element.59), channel_id=1, source_target_pairs={{0,1},{1,0},{2,3},{3,2},{4,5},{5,4},{6,7},{7,6},{8,9},{9,8},{10,11... | collective-permute-start | bytes 1081352 | tf_op jit(solution)/shard_map/ppermute | solution.py:23
  32.2 12.3 %collective-permute-start.5 = (bf16[22,64,128]{2,1,0:T(8,128)(2,1)S(1)}, bf16[22,64,128]{2,1,0:T(8,128)(2,1)S(1)}, u32[]{:S(2)}, u32[]{:S(2)}) collective-permute-start(bf16[22,64,128]{2,1,0:T(8,128)(2,1)S(1)} %get-tuple-element.58), channel_id=1, source_target_pairs={{0,2},{1,3},{2,0},{3,1},{4,6},{5,7},{6,4},{7,5},{8,10},{9,11},{10,... | collective-permute-start | bytes 1081352 | tf_op jit(solution)/shard_map/ppermute | solution.py:23
  34.0 13.2 %collective-permute-start.7 = (bf16[22,64,128]{2,1,0:T(8,128)(2,1)S(1)}, bf16[22,64,128]{2,1,0:T(8,128)(2,1)S(1)}, u32[]{:S(2)}, u32[]{:S(2)}) collective-permute-start(bf16[22,64,128]{2,1,0:T(8,128)(2,1)S(1)} %level1_0_0.1.refs_5_.refs_2_), channel_id=1, source_target_pairs={{0,16},{1,17},{2,18},{3,19},{4,20},{5,21},{6,22},{7,23},{8,24},{9,... | collective-permute-start | bytes 1081352 | tf_op jit(solution)/shard_map/ppermute | solution.py:23
  36.7 11.6 %collective-permute-start.10 = (bf16[22,64,128]{2,1,0:T(8,128)(2,1)S(1)}, bf16[22,64,128]{2,1,0:T(8,128)(2,1)S(1)}, u32[]{:S(2)}, u32[]{:S(2)}) collective-permute-start(bf16[22,64,128]{2,1,0:T(8,128)(2,1)S(1)} %get-tuple-element.62), channel_id=1, source_target_pairs={{0,1},{1,0},{2,3},{3,2},{4,5},{5,4},{6,7},{7,6},{8,9},{9,8},{10,11... | collective-permute-start | bytes 1081352 | tf_op jit(solution)/shard_map/ppermute | solution.py:23
  41.9 10.3 %collective-permute-start.11 = (bf16[22,64,128]{2,1,0:T(8,128)(2,1)S(1)}, bf16[22,64,128]{2,1,0:T(8,128)(2,1)S(1)}, u32[]{:S(2)}, u32[]{:S(2)}) collective-permute-start(bf16[22,64,128]{2,1,0:T(8,128)(2,1)S(1)} %get-tuple-element.64), channel_id=1, source_target_pairs={{0,2},{1,3},{2,0},{3,1},{4,6},{5,7},{6,4},{7,5},{8,10},{9,11},{10,... | collective-permute-start | bytes 1081352 | tf_op jit(solution)/shard_map/ppermute | solution.py:23
  42.0 10.2 %collective-permute-start.8 = (bf16[22,64,128]{2,1,0:T(8,128)(2,1)S(1)}, bf16[22,64,128]{2,1,0:T(8,128)(2,1)S(1)}, u32[]{:S(2)}, u32[]{:S(2)}) collective-permute-start(bf16[22,64,128]{2,1,0:T(8,128)(2,1)S(1)} %level1_0_1.1.refs_4_.refs_3_), channel_id=1, source_target_pairs={{0,16},{1,17},{2,18},{3,19},{4,20},{5,21},{6,22},{7,23},{8,24},{9,... | collective-permute-start | bytes 1081352 | tf_op jit(solution)/shard_map/ppermute | solution.py:23
  44.5 8.9 %collective-permute-start.9 = (bf16[22,64,128]{2,1,0:T(8,128)(2,1)S(1)}, bf16[22,64,128]{2,1,0:T(8,128)(2,1)S(1)}, u32[]{:S(2)}, u32[]{:S(2)}) collective-permute-start(bf16[22,64,128]{2,1,0:T(8,128)(2,1)S(1)} %get-tuple-element.61), channel_id=1, source_target_pairs={{0,1},{1,0},{2,3},{3,2},{4,5},{5,4},{6,7},{7,6},{8,9},{9,8},{10,11... | collective-permute-start | bytes 1081352 | tf_op jit(solution)/shard_map/ppermute | solution.py:23
  49.6 11.0 %collective-permute-start.13 = (bf16[22,64,128]{2,1,0:T(8,128)(2,1)S(1)}, bf16[22,64,128]{2,1,0:T(8,128)(2,1)S(1)}, u32[]{:S(2)}, u32[]{:S(2)}) collective-permute-start(bf16[22,64,128]{2,1,0:T(8,128)(2,1)S(1)} %get-tuple-element.68), channel_id=1, source_target_pairs={{0,2},{1,3},{2,0},{3,1},{4,6},{5,7},{6,4},{7,5},{8,10},{9,11},{10,... | collective-permute-start | bytes 1081352 | tf_op jit(solution)/shard_map/ppermute | solution.py:23
  49.8 10.8 %collective-permute-start.12 = (bf16[22,64,128]{2,1,0:T(8,128)(2,1)S(1)}, bf16[22,64,128]{2,1,0:T(8,128)(2,1)S(1)}, u32[]{:S(2)}, u32[]{:S(2)}) collective-permute-start(bf16[22,64,128]{2,1,0:T(8,128)(2,1)S(1)} %level1_0_2.1.refs_5_.refs_4_), channel_id=1, source_target_pairs={{0,16},{1,17},{2,18},{3,19},{4,20},{5,21},{6,22},{7,23},{8,24},{9,... | collective-permute-start | bytes 1081352 | tf_op jit(solution)/shard_map/ppermute | solution.py:23
  54.6 15.7 %collective-permute-start.15 = (bf16[22,64,128]{2,1,0:T(8,128)(2,1)S(1)}, bf16[22,64,128]{2,1,0:T(8,128)(2,1)S(1)}, u32[]{:S(2)}, u32[]{:S(2)}) collective-permute-start(bf16[22,64,128]{2,1,0:T(8,128)(2,1)S(1)} %get-tuple-element.71), channel_id=1, source_target_pairs={{0,2},{1,3},{2,0},{3,1},{4,6},{5,7},{6,4},{7,5},{8,10},{9,11},{10,... | collective-permute-start | bytes 1081352 | tf_op jit(solution)/shard_map/ppermute | solution.py:23
  54.8 15.6 %collective-permute-start.16 = (bf16[22,64,128]{2,1,0:T(8,128)(2,1)S(1)}, bf16[22,64,128]{2,1,0:T(8,128)(2,1)S(1)}, u32[]{:S(2)}, u32[]{:S(2)}) collective-permute-start(bf16[22,64,128]{2,1,0:T(8,128)(2,1)S(1)} %level1_1_0.1.refs_5_.refs_2_), channel_id=1, source_target_pairs={{0,16},{1,17},{2,18},{3,19},{4,20},{5,21},{6,22},{7,23},{8,24},{9,... | collective-permute-start | bytes 1081352 | tf_op jit(solution)/shard_map/ppermute | solution.py:23
  65.4 18.0 %collective-permute-start.14 = (bf16[32,64,128]{2,1,0:T(8,128)(2,1)S(1)}, bf16[32,64,128]{2,1,0:T(8,128)(2,1)S(1)}, u32[]{:S(2)}, u32[]{:S(2)}) collective-permute-start(bf16[32,64,128]{2,1,0:T(8,128)(2,1)S(1)} %get-tuple-element.70), channel_id=1, source_target_pairs={{0,32},{32,0},{64,96},{96,64},{1,33},{33,1},{65,97},{97,65},{2,34}... | collective-permute-start | bytes 1572872 | tf_op jit(solution)/shard_map/ppermute | solution.py:23
  70.1 11.5 %collective-permute-start.17 = (bf16[22,64,128]{2,1,0:T(8,128)(2,1)S(1)}, bf16[22,64,128]{2,1,0:T(8,128)(2,1)S(1)}, u32[]{:S(2)}, u32[]{:S(2)}) collective-permute-start(bf16[22,64,128]{2,1,0:T(8,128)(2,1)S(1)} %level1_1_1.1.refs_6_.refs_3_), channel_id=1, source_target_pairs={{0,16},{1,17},{2,18},{3,19},{4,20},{5,21},{6,22},{7,23},{8,24},{9,... | collective-permute-start | bytes 1081352 | tf_op jit(solution)/shard_map/ppermute | solution.py:23
  71.6 17.8 %collective-permute-start.19 = (bf16[22,64,128]{2,1,0:T(8,128)(2,1)S(1)}, bf16[22,64,128]{2,1,0:T(8,128)(2,1)S(1)}, u32[]{:S(2)}, u32[]{:S(2)}) collective-permute-start(bf16[22,64,128]{2,1,0:T(8,128)(2,1)S(1)} %level1_1_2.1.refs_4_.refs_7_), channel_id=1, source_target_pairs={{0,16},{1,17},{2,18},{3,19},{4,20},{5,21},{6,22},{7,23},{8,24},{9,... | collective-permute-start | bytes 1081352 | tf_op jit(solution)/shard_map/ppermute | solution.py:23
  83.5 8.8 %collective-permute-start.18 = (bf16[16,64,128]{2,1,0:T(8,128)(2,1)S(1)}, bf16[16,64,128]{2,1,0:T(8,128)(2,1)S(1)}, u32[]{:S(2)}, u32[]{:S(2)}) collective-permute-start(bf16[16,64,128]{2,1,0:T(8,128)(2,1)S(1)} %get-tuple-element.74.refs_6_), channel_id=1, source_target_pairs={{0,64},{32,96},{64,0},{96,32},{1,65},{33,97},{65,1},{97,33},{2,66}... | collective-permute-start | bytes 786440 | tf_op jit(solution)/shard_map/ppermute | solution.py:23
  91.5 2.3 %collective-permute-start.21 = (bf16[16,64,128]{2,1,0:T(8,128)(2,1)S(1)}, bf16[16,64,128]{2,1,0:T(8,128)(2,1)S(1)}, u32[]{:S(2)}, u32[]{:S(2)}) collective-permute-start(bf16[16,64,128]{2,1,0:T(8,128)(2,1)S(1)} %get-tuple-element.80), channel_id=1, source_target_pairs={{0,32},{32,0},{64,96},{96,64},{1,33},{33,1},{65,97},{97,65},{2,34}... | collective-permute-start | bytes 786440 | tf_op jit(solution)/shard_map/ppermute | solution.py:23
  93.8 8.0 %collective-permute-start.22 = (bf16[16,64,128]{2,1,0:T(8,128)(2,1)S(1)}, bf16[16,64,128]{2,1,0:T(8,128)(2,1)S(1)}, u32[]{:S(2)}, u32[]{:S(2)}) collective-permute-start(bf16[16,64,128]{2,1,0:T(8,128)(2,1)S(1)} %join_1_0.1), channel_id=1, source_target_pairs={{0,64},{32,96},{64,0},{96,32},{1,65},{33,97},{65,1},{97,33},{2,66}... | collective-permute-start | bytes 786440 | tf_op jit(solution)/shard_map/ppermute | solution.py:23
  94.7 7.2 %collective-permute-start.20 = (bf16[16,64,128]{2,1,0:T(8,128)(2,1)S(1)}, bf16[16,64,128]{2,1,0:T(8,128)(2,1)S(1)}, u32[]{:S(2)}, u32[]{:S(2)}) collective-permute-start(bf16[16,64,128]{2,1,0:T(8,128)(2,1)S(1)} %get-tuple-element.79), channel_id=1, source_target_pairs={{0,32},{32,0},{64,96},{96,64},{1,33},{33,1},{65,97},{97,65},{2,34}... | collective-permute-start | bytes 786440 | tf_op jit(solution)/shard_map/ppermute | solution.py:23

commit v2 on v1

--- a/solution.py
+++ b/solution.py
@@ -68,6 +68,7 @@
 
 
 def pad(out, used):
+    return
     for i in range(used, out.shape[0]):
         out[i] = jnp.zeros(out.shape[1:], out.dtype)
 
@@ -80,15 +81,9 @@
     pad(out, zed[k + 1] - zed[k])
 
 
-def head_kernel(first, pm_hbm, x_hbm, walk, x0, *rest):
-    zouts, (pm, seen, sem) = rest[: len(first)], rest[len(first):]
-    maps = pltpu.make_async_copy(pm_hbm, pm, sem.at[0])
-    data = pltpu.make_async_copy(x_hbm, x0, sem.at[1])
-    maps.start()
-    data.start()
+def walk_cycles(pm, seen, walk, count):
     for i in range(NB):
         seen[i] = 0
-    maps.wait()
 
     def step(p, carry):
         cur, start, begin, scan = carry
@@ -111,14 +106,38 @@
         return cur, start, begin, scan
 
     zero = jnp.int32(0)
-    lax.fori_loop(0, NB, step, (zero, zero, zero, zero))
+    lax.fori_loop(0, count, step, (zero, zero, zero, zero))
+
+
+def gather_first(pm, walk, x0, out, piece, k):
+    r0, rows, sizes = PIECES[piece]
+    _, zed = bounds(sizes)
+    for q in range(zed[k], zed[k + 1]):
+        out[q - zed[k]] = x0[pm[0, walk[CYC, q]], pl.ds(r0, rows), :]
+    pad(out, zed[k + 1] - zed[k])
+
+
+def head_kernel(pm_hbm, x_hbm, pm, x0, out, walk, seen, sem):
+    maps = pltpu.make_async_copy(pm_hbm, pm, sem.at[0])
+    data = pltpu.make_async_copy(x_hbm, x0, sem.at[1])
+    maps.start()
+    data.start()
+    maps.wait()
+    walk_cycles(pm, seen, walk, bounds(PIECES[0][2])[1][1])
     data.wait()
-    for (piece, k), out in zip(first, zouts):
-        r0, rows, sizes = PIECES[piece]
-        _, zed = bounds(sizes)
-        for q in range(zed[k], zed[k + 1]):
-            out[q - zed[k]] = x0[pm[0, walk[CYC, q]], pl.ds(r0, rows), :]
-        pad(out, zed[k + 1] - zed[k])
+    gather_first(pm, walk, x0, out, 0, 0)
+
+
+def next_kernel(chunks, pm, x0, d_ref, o_ref, walk, w_ref, *rest):
+    outs, (seen, sem) = rest[: len(chunks)], rest[len(chunks):]
+    copies = load_copies(0, d_ref, o_ref, w_ref, sem)
+    for copy in copies:
+        copy.start()
+    walk_cycles(pm, seen, walk, NB)
+    for (piece, k), out in zip(chunks, outs):
+        gather_first(pm, walk, x0, out, piece, k)
+    for copy in copies:
+        copy.wait()
 
 
 def load_copies(level, d_ref, o_ref, w_ref, sem):
@@ -129,10 +148,10 @@
 
 
 def tables_kernel(pm, walk, d_ref, o_ref, order, *refs):
-    w_refs, (inv, sem) = refs[:4], refs[4:]
+    w_refs, (inv, sem) = refs[:-2], refs[-2:]
     copies = []
-    for level in range(4):
-        copies += load_copies(level, d_ref, o_ref, w_refs[level], sem.at[level])
+    for i, w_ref in enumerate(w_refs):
+        copies += load_copies(i + 1, d_ref, o_ref, w_ref, sem.at[i])
     for copy in copies:
         copy.start()
 
@@ -210,26 +229,18 @@
             x3[edge[k] + i] = mm(cat(x2[order[POS, j]], got[k][i]), factors(w, j)).astype(BF)
 
 
-def products(order, w3, full, quarter, out, base):
+def products(order, w3, full, quarters, outs):
     q = NB // 4
-    for i in range(q):
-        j = quarter * q + i
-        other = order[PM3, j]
-        total = mm(cat(full[j], full[other]), cat(w3[0, j], w3[1, other]))
-        out[base + i] = total.astype(out.dtype)
-
-
-def near_far(order, w3, full, send, keep, far, near):
-    me = lax.axis_index("hi")
-    z, core = me // 2, me % 2
-    base = 0
-    for chip in ([1 - z] if far else []) + ([z] if near else []):
-        products(order, w3, full, 2 * chip + 1 - core, send, base)
-        products(order, w3, full, 2 * chip + core, keep, base)
-        base += NB // 4
-
-
-def late_kernel(piece, near, order, w, w3, x2, x3, got, send, keep, full):
+    for quarter, out in zip(quarters, outs):
+        for i in range(q):
+            j = quarter * q + i
+            other = order[PM3, j]
+            total = mm(cat(full[j], full[other]), cat(w3[0, j], w3[1, other]))
+            ref = out[i // out[0].shape[0]]
+            ref[i % out[0].shape[0]] = total.astype(ref.dtype)
+
+
+def late_kernel(piece, order, w, w3, x2, x3, got, send, keep, full):
     _, _, sizes = PIECES[piece]
     edge, _ = bounds(sizes)
     last = edge[-2]
@@ -238,30 +249,33 @@
     for i in range(sizes[-1]):
         j = order[TJ, last + i]
         full[j] = mm(cat(x2[order[POS, j]], got[i]), factors(w, j)).astype(BF)
-    near_far(order, w3, full, send, keep, True, near)
-
-
-def rest_kernel(order, w3, full, send, keep):
-    near_far(order, w3, full, send, keep, False, True)
-
-
-def join_kernel(keep, got, send, own=None):
-    q = NB // 4
-    send[...] = (keep[:q] + got[:q].astype(F32)).astype(BF)
-    if own is not None:
-        own[...] = (keep[q:] + got[q:].astype(F32))
+    me = lax.axis_index("hi")
+    z, core = me // 2, me % 2
+    products(order, w3, full, (2 * (1 - z) + 1 - core, 2 * (1 - z) + core), ([send], [keep]))
+
+
+def rest_kernel(order, w3, full, *outs):
+    *sends, keep = outs
+    me = lax.axis_index("hi")
+    z, core = me // 2, me % 2
+    products(order, w3, full, (2 * z + 1 - core, 2 * z + core), (sends, [keep]))
+
+
+def join_kernel(keep, got, send):
+    send[...] = (keep[...] + got[...].astype(F32)).astype(BF)
 
 
 def final_kernel(*refs):
-    out = refs[-1]
+    refs, out = list(refs[:-1]), refs[-1]
     for piece, (r0, rows, _) in enumerate(PIECES):
-        if piece < len(PIECES) - 1:
-            own = refs[2 * piece][...]
-            far = refs[2 * piece + 1]
-        else:
-            own = refs[2 * piece][...] + refs[2 * piece + 1][...].astype(F32)
-            far = refs[2 * piece + 2]
-        out[:, pl.ds(r0, rows), :] = (own + far[...].astype(F32)).astype(BF)
+        far, own, *cores = refs[: 3 + piece]
+        del refs[: 3 + piece]
+        base = 0
+        for core in cores:
+            part = pl.ds(base, core.shape[0])
+            base += core.shape[0]
+            total = own[part] + core[...].astype(F32) + far[part].astype(F32)
+            out[part, pl.ds(r0, rows), :] = total.astype(BF)
 
 
 def plan():
@@ -273,8 +287,8 @@
         if s:
             steps.append(("level1", *chunks[s - 1]))
     last = steps.pop()
-    steps += [("early", 0, 0), last, ("late", 0, 0), ("level1", *chunks[-1])]
-    steps += [("early", 1, 0), ("join", 0, 0), ("late", 1, 0), ("rest", 1, 0), ("join", 1, 0)]
+    steps += [last, ("early", 0, 0), ("late", 0, 0), ("rest", 0, 0), ("level1", *chunks[-1])]
+    steps += [("early", 1, 0), ("join", 0, 0), ("late", 1, 0), ("join", 1, 0), ("rest", 1, 0)]
     return chunks, steps
 
 
@@ -284,35 +298,47 @@
     chunks, steps = plan()
 
     def zshape(piece, k):
-        return pltpu.VMEM((slots(piece), PIECES[piece][1], P_), BF)
+        _, zed = bounds(PIECES[piece][2])
+        return pltpu.VMEM((zed[k + 1] - zed[k], PIECES[piece][1], P_), BF)
 
     first = chunks[: DEPTH + 1]
-    walk, x0, *zmsg = call(
-        functools.partial(head_kernel, first),
+    wshape = pltpu.VMEM((2, NB, P_, P_), BF)
+    pm, x0, zmsg = call(
+        head_kernel,
         "head",
-        [jax.ShapeDtypeStruct((3, NB), jnp.int32), pltpu.VMEM((NB, P_, P_), BF)]
-        + [zshape(*c) for c in first],
+        [pltpu.SMEM((4, NB), jnp.int32), pltpu.VMEM((NB, P_, P_), BF), zshape(*first[0])],
         [hbm(maps), blocks],
         [ANY, ANY],
         (),
-        scratch=[pltpu.SMEM((4, NB), jnp.int32), pltpu.SMEM((NB,), jnp.int32), pltpu.SemaphoreType.DMA((2,))],
-        out_specs=[SM] + [VM] * (1 + len(first)),
+        scratch=[pltpu.SMEM((3, NB), jnp.int32), pltpu.SMEM((NB,), jnp.int32), pltpu.SemaphoreType.DMA((2,))],
+        out_specs=[SM, VM, VM],
     )
+    walk, w0, *more = call(
+        functools.partial(next_kernel, first[1:]),
+        "next",
+        [pltpu.SMEM((3, NB), jnp.int32), wshape] + [zshape(*c) for c in first[1:]],
+        [pm, x0, diag, off],
+        [SM, VM, ANY, ANY],
+        (),
+        scratch=[pltpu.SMEM((NB,), jnp.int32), pltpu.SemaphoreType.DMA((2,))],
+        out_specs=[SM] + [VM] * len(first),
+    )
+    zmsg = [zmsg] + more
     zin = {c: partner_2(m, "lo", 0) for c, m in zip(first, zmsg)}
-    wshape = pltpu.VMEM((2, NB, P_, P_), BF)
     order, *w = call(
         tables_kernel,
         "tables",
-        [jax.ShapeDtypeStruct((8, NB), jnp.int32)] + [wshape] * 4,
-        [maps, walk, diag, off],
+        [pltpu.SMEM((8, NB), jnp.int32)] + [wshape] * 3,
+        [pm, walk, diag, off],
         [SM, SM, ANY, ANY],
-        (x0,),
-        scratch=[pltpu.SMEM((NB,), jnp.int32), pltpu.SemaphoreType.DMA((4, 2))],
-        out_specs=[SM] + [VM] * 4,
+        (w0,),
+        scratch=[pltpu.SMEM((NB,), jnp.int32), pltpu.SemaphoreType.DMA((3, 2))],
+        out_specs=[SM] + [VM] * 3,
     )
+    w = [w0, *w]
     dep = x0
     top = lax.axis_size("lo").bit_length() - 1
-    xs, yin, x2, xin, early, late, core, chip = {}, {}, {}, {}, {}, {}, {}, {}
+    xs, yin, x2, xin, early, late, core, chip, far = {}, {}, {}, {}, {}, {}, {}, {}, {}
     for kind, piece, k in steps:
         _, rows, sizes = PIECES[piece]
         c = (piece, k)
@@ -321,8 +347,10 @@
         part = lambda count, dtype: pltpu.VMEM((count, rows, P_), dtype)
         if kind == "level0":
             s = chunks.index(c)
+            if s > 2:
+                dep = (*dep, xin[chunks[s - 3]])
             after = chunks[s + DEPTH] if 0 < s < len(chunks) - DEPTH else None
-            outs = [part(sizes[k] + 2, BF), part(slots(piece), BF)]
+            outs = [part(sizes[k] + 2, BF), part(sizes[k], BF)]
             outs += [zshape(*after)] if after else []
             ins = [order, x0, zin[c], w[0]] + ([xs[piece, k - 1]] if k else [])
             specs = [SM] + [VM] * (len(ins) - 1)
@@ -335,12 +363,9 @@
                 zin[after] = partner_2(more[0], "lo", 0)
             dep = xs[c]
         elif kind == "level1":
-            s = chunks.index(c) - 2
-            if s >= 0:
-                dep = (*dep, xin[chunks[s]])
             (x2[c],) = call(
                 functools.partial(level1_kernel, piece, k),
-                name, [part(slots(piece), BF)],
+                name, [part(sizes[k], BF)],
                 [order, xs[c], yin[c], w[1]], [SM, VM, VM, VM], dep,
             )
             xin[c] = partner_2(x2[c], "lo", top - 1)
@@ -355,33 +380,34 @@
             )
             dep = early[piece][0]
         elif kind == "late":
-            split = piece == len(PIECES) - 1
-            count = NB // 4 if split else NB // 2
+            if piece:
+                dep = (*dep, *chip[piece - 1][1:])
             send, keep, full = call(
-                functools.partial(late_kernel, piece, not split),
-                name, [part(count, BF), part(count, F32), part(NB, BF)],
+                functools.partial(late_kernel, piece),
+                name, [part(NB // 4, BF), part(NB // 4, F32), part(NB, BF)],
                 [order, w[2], w[3], *early[piece], xin[piece, len(sizes) - 1]], [SM] + [VM] * 5, dep,
             )
             late[piece] = full
             core[piece] = keep, partner_2(send, "hi", 0)
             dep = keep
         elif kind == "rest":
-            if piece:
-                dep = (*dep, chip[piece - 1][1])
-            send, keep = call(
+            if not piece:
+                dep = (*dep, xin[chunks[-3]])
+            count = 1 + piece
+            *sends, keep = call(
                 rest_kernel,
-                name, [part(NB // 4, BF), part(NB // 4, F32)],
+                name, [part(NB // 4 // count, BF)] * count + [part(NB // 4, F32)],
                 [order, w[3], late[piece]], [SM, VM, VM], dep,
             )
-            chip[piece] = keep, partner_2(send, "hi", 0)
+            chip[piece] = keep, *[partner_2(send, "hi", 0) for send in sends]
             dep = keep
         else:
-            split = piece == len(PIECES) - 1
-            outs = [part(NB // 4, BF)] + ([] if split else [part(NB // 4, F32)])
-            send, *own = call(join_kernel, name, outs, [*core[piece]], [VM, VM], dep)
-            chip[piece] = *(chip[piece] if split else own), partner_2(send, "hi", 1)
+            if piece:
+                dep = (*dep, far[piece - 1])
+            (send,) = call(join_kernel, name, [part(NB // 4, BF)], [*core[piece]], [VM, VM], dep)
+            far[piece] = partner_2(send, "hi", 1)
             dep = send
-    ins = [a for piece in range(len(PIECES)) for a in chip[piece]]
+    ins = [a for piece in range(len(PIECES)) for a in (far[piece], *chip[piece])]
     (out,) = call(
         final_kernel, "final", [jax.ShapeDtypeStruct((NB // 4, P_, P_), BF)],
         ins, [VM] * len(ins), (),

time: 103 us -> 89.7 us (0.87)
  Pallas kernels: 36.8 us -> 23.9 us
  waiting for transfers between devices: 22.5 us -> 13.4 us
  starting transfers between devices: 42.6 us -> 51.3 us
    pallas_call x22 -> x24, Pallas kernels: 36.8 us -> 23.9 us  [call(): pl.pallas_call(run, out_shape=outs, in_specs=list(specs) + [ANY] * len(ex...]
    ppermute x23 -> x25, waiting for transfers between devices: 22.5 us -> 13.4 us  [partner_2(): lax.ppermute(array, axis, [(i, i ^ 1 << apart) for i in range(lax.axis_si...]
    ppermute x23 -> x25, starting transfers between devices: 42.6 us -> 51.3 us  [partner_2(): lax.ppermute(array, axis, [(i, i ^ 1 << apart) for i in range(lax.axis_si...]
  transfers between devices with their start and end apart: 23 -> 25, of which waited for: 6 -> 10; matrix products, arithmetic and copies ran while one was open for 0% -> 0% of each run, Pallas kernels for 32% -> 24%
where the time goes in v2:
time: 89.7 us; the launch traced here: 88.7 us
  starting transfers between devices  51.3 us (57%)
  Pallas kernels  23.9 us (27%)
  waiting for transfers between devices  13.4 us (15%)
    ppermute x25, starting transfers between devices, partner_2(): lax.ppermute(array, axis, [(i, i ^ 1 << apart) for i in range(lax.axis_si...  51.3 us
    pallas_call x24, Pallas kernels, call(): pl.pallas_call(run, out_shape=outs, in_specs=list(specs) + [ANY] * len(ex...  23.9 us
    ppermute x25, waiting for transfers between devices, partner_2(): lax.ppermute(array, axis, [(i, i ^ 1 << apart) for i in range(lax.axis_si...  13.4 us
  transfers between devices with their start and end apart: 25, of which 10 were waited for; matrix products, arithmetic and copies ran while one was open for 0% of the time, Pallas kernels for 24%

profile of v2, /device:TPU:1, one launch (start us, length us, event | category | flops | bytes accessed | tf_op | source)
XLA Modules:
  0.0 88.7 jit_solution(13409634900382005305)
XLA Ops:
  0.0 1.6 %head.1 = (s32[4,64]{1,0:T(4,128)S(4)}, bf16[64,128,128]{2,1,0:T(8,128)(2,1)S(1)}, bf16[22,64,128]{2,1,0:T(8,128)(2,1)S(1)}) custom-call(s32[4,64]{1,0:T(4,128)} %refs_0_.1, bf16[64,128,128]{2,1,0:T(8,128)(2,1)} %refs_1_.1), custom_call_target="tpu_custom_call" | custom-call | bytes 2000000 | tf_op jit(solution)/shard_map/head/pallas_call | solution.py:44
  1.6 4.5 %collective-permute-start = (bf16[22,64,128]{2,1,0:T(8,128)(2,1)S(1)}, bf16[22,64,128]{2,1,0:T(8,128)(2,1)S(1)}, u32[]{:S(2)}, u32[]{:S(2)}) collective-permute-start(bf16[22,64,128]{2,1,0:T(8,128)(2,1)S(1)} %get-tuple-element.53), channel_id=1, source_target_pairs={{0,1},{1,0},{2,3},{3,2},{4,5},{5,4},{6,7},{7,6},{8,9},{9,8},{10,11... | collective-permute-start | bytes 1081352 | tf_op jit(solution)/shard_map/ppermute | solution.py:23
  6.1 2.2 %next.1 = (s32[3,64]{1,0:T(4,128)S(4)}, bf16[2,64,128,128]{3,2,1,0:T(8,128)(2,1)S(1)}, bf16[22,64,128]{2,1,0:T(8,128)(2,1)S(1)}, bf16[20,64,128]{2,1,0:T(8,128)(2,1)S(1)}) custom-call(s32[4,64]{1,0:T(4,128)S(4)} %get-tuple-element.46.refs_0_, bf16[64,128,128]{2,1,0:T(8,128)(2,1)S(1)} %get-tuple-element.47.refs_1_.refs_4_, bf16[4,64,128,128]{3,2,1,0:T(8,128)(2,1)} %refs_2_.3, ...), custom_call_target="tpu_custom_call" | custom-call | bytes 2000000 | tf_op jit(solution)/shard_map/next/pallas_call | solution.py:44
  8.5 4.7 %tables.1 = (s32[8,64]{1,0:T(8,128)S(4)}, bf16[2,64,128,128]{3,2,1,0:T(8,128)(2,1)S(1)}, bf16[2,64,128,128]{3,2,1,0:T(8,128)(2,1)S(1)}, bf16[2,64,128,128]{3,2,1,0:T(8,128)(2,1)S(1)}) custom-call(s32[4,64]{1,0:T(4,128)S(4)} %get-tuple-element.46.refs_0_, s32[3,64]{1,0:T(4,128)S(4)} %get-tuple-element.48.refs_1_, bf16[4,64,128,128]{3,2,1,0:T(8,128)(2,1)} %refs_2_.3, ...), custom_call_target="tpu_custom_call" | custom-call | bytes 2000000 | tf_op jit(solution)/shard_map/tables/pallas_call | solution.py:44
  13.2 1.1 %collective-permute-done.refs_2_ = bf16[22,64,128]{2,1,0:T(8,128)(2,1)S(1)} collective-permute-done((bf16[22,64,128]{2,1,0:T(8,128)(2,1)S(1)}, bf16[22,64,128]{2,1,0:T(8,128)(2,1)S(1)}, u32[]{:S(2)}, u32[]{:S(2)}) %collective-permute-start) | collective-permute-done | bytes 360480 | tf_op jit(solution)/shard_map/ppermute | solution.py:23
  14.9 1.4 %collective-permute-start.1 = (bf16[21,64,128]{2,1,0:T(8,128)(2,1)S(1)}, bf16[21,64,128]{2,1,0:T(8,128)(2,1)S(1)}, u32[]{:S(2)}, u32[]{:S(2)}) collective-permute-start(bf16[21,64,128]{2,1,0:T(8,128)(2,1)S(1)} %get-tuple-element.56), channel_id=1, source_target_pairs={{0,2},{1,3},{2,0},{3,1},{4,6},{5,7},{6,4},{7,5},{8,10},{9,11},{10,... | collective-permute-start | bytes 1032200 | tf_op jit(solution)/shard_map/ppermute | solution.py:23
  16.3 2.6 %collective-permute-start.4 = (bf16[20,64,128]{2,1,0:T(8,128)(2,1)S(1)}, bf16[20,64,128]{2,1,0:T(8,128)(2,1)S(1)}, u32[]{:S(2)}, u32[]{:S(2)}) collective-permute-start(bf16[20,64,128]{2,1,0:T(8,128)(2,1)S(1)} %get-tuple-element.60), channel_id=1, source_target_pairs={{0,1},{1,0},{2,3},{3,2},{4,5},{5,4},{6,7},{7,6},{8,9},{9,8},{10,11... | collective-permute-start | bytes 983048 | tf_op jit(solution)/shard_map/ppermute | solution.py:23
  19.0 3.1 %collective-permute-done.2.refs_2_ = bf16[22,64,128]{2,1,0:T(8,128)(2,1)S(1)} collective-permute-done((bf16[22,64,128]{2,1,0:T(8,128)(2,1)S(1)}, bf16[22,64,128]{2,1,0:T(8,128)(2,1)S(1)}, u32[]{:S(2)}, u32[]{:S(2)}) %collective-permute-start.2) | collective-permute-done | bytes 360480 | tf_op jit(solution)/shard_map/ppermute | solution.py:23
  22.7 1.4 %collective-permute-start.3 = (bf16[22,64,128]{2,1,0:T(8,128)(2,1)S(1)}, bf16[22,64,128]{2,1,0:T(8,128)(2,1)S(1)}, u32[]{:S(2)}, u32[]{:S(2)}) collective-permute-start(bf16[22,64,128]{2,1,0:T(8,128)(2,1)S(1)} %get-tuple-element.59), channel_id=1, source_target_pairs={{0,2},{1,3},{2,0},{3,1},{4,6},{5,7},{6,4},{7,5},{8,10},{9,11},{10,... | collective-permute-start | bytes 1081352 | tf_op jit(solution)/shard_map/ppermute | solution.py:23
  24.0 2.6 %collective-permute-start.6 = (bf16[22,64,128]{2,1,0:T(8,128)(2,1)S(1)}, bf16[22,64,128]{2,1,0:T(8,128)(2,1)S(1)}, u32[]{:S(2)}, u32[]{:S(2)}) collective-permute-start(bf16[22,64,128]{2,1,0:T(8,128)(2,1)S(1)} %get-tuple-element.63), channel_id=1, source_target_pairs={{0,1},{1,0},{2,3},{3,2},{4,5},{5,4},{6,7},{7,6},{8,9},{9,8},{10,11... | collective-permute-start | bytes 1081352 | tf_op jit(solution)/shard_map/ppermute | solution.py:23
  27.3 2.8 %collective-permute-start.7 = (bf16[21,64,128]{2,1,0:T(8,128)(2,1)S(1)}, bf16[21,64,128]{2,1,0:T(8,128)(2,1)S(1)}, u32[]{:S(2)}, u32[]{:S(2)}) collective-permute-start(bf16[21,64,128]{2,1,0:T(8,128)(2,1)S(1)} %level1_0_0.1.refs_5_.refs_2_), channel_id=1, source_target_pairs={{0,16},{1,17},{2,18},{3,19},{4,20},{5,21},{6,22},{7,23},{8,24},{9,... | collective-permute-start | bytes 1032200 | tf_op jit(solution)/shard_map/ppermute | solution.py:23
  31.0 2.6 %collective-permute-start.9 = (bf16[22,64,128]{2,1,0:T(8,128)(2,1)S(1)}, bf16[22,64,128]{2,1,0:T(8,128)(2,1)S(1)}, u32[]{:S(2)}, u32[]{:S(2)}) collective-permute-start(bf16[22,64,128]{2,1,0:T(8,128)(2,1)S(1)} %get-tuple-element.65), channel_id=1, source_target_pairs={{0,1},{1,0},{2,3},{3,2},{4,5},{5,4},{6,7},{7,6},{8,9},{9,8},{10,11... | collective-permute-start | bytes 1081352 | tf_op jit(solution)/shard_map/ppermute | solution.py:23
  34.3 2.8 %collective-permute-start.8 = (bf16[22,64,128]{2,1,0:T(8,128)(2,1)S(1)}, bf16[22,64,128]{2,1,0:T(8,128)(2,1)S(1)}, u32[]{:S(2)}, u32[]{:S(2)}) collective-permute-start(bf16[22,64,128]{2,1,0:T(8,128)(2,1)S(1)} %level1_0_1.1.refs_4_.refs_3_), channel_id=1, source_target_pairs={{0,16},{1,17},{2,18},{3,19},{4,20},{5,21},{6,22},{7,23},{8,24},{9,... | collective-permute-start | bytes 1081352 | tf_op jit(solution)/shard_map/ppermute | solution.py:23
  39.4 2.8 %collective-permute-start.13 = (bf16[21,64,128]{2,1,0:T(8,128)(2,1)S(1)}, bf16[21,64,128]{2,1,0:T(8,128)(2,1)S(1)}, u32[]{:S(2)}, u32[]{:S(2)}) collective-permute-start(bf16[21,64,128]{2,1,0:T(8,128)(2,1)S(1)} %level1_0_2.1.refs_5_.refs_4_), channel_id=1, source_target_pairs={{0,16},{1,17},{2,18},{3,19},{4,20},{5,21},{6,22},{7,23},{8,24},{9,... | collective-permute-start | bytes 1032200 | tf_op jit(solution)/shard_map/ppermute | solution.py:23
  42.2 2.6 %collective-permute-start.11 = (bf16[20,64,128]{2,1,0:T(8,128)(2,1)S(1)}, bf16[20,64,128]{2,1,0:T(8,128)(2,1)S(1)}, u32[]{:S(2)}, u32[]{:S(2)}) collective-permute-start(bf16[20,64,128]{2,1,0:T(8,128)(2,1)S(1)} %get-tuple-element.68), channel_id=1, source_target_pairs={{0,1},{1,0},{2,3},{3,2},{4,5},{5,4},{6,7},{7,6},{8,9},{9,8},{10,11... | collective-permute-start | bytes 983048 | tf_op jit(solution)/shard_map/ppermute | solution.py:23
  46.8 3.1 %collective-permute-start.16 = (bf16[21,64,128]{2,1,0:T(8,128)(2,1)S(1)}, bf16[21,64,128]{2,1,0:T(8,128)(2,1)S(1)}, u32[]{:S(2)}, u32[]{:S(2)}) collective-permute-start(bf16[21,64,128]{2,1,0:T(8,128)(2,1)S(1)} %level1_1_0.1.refs_5_.refs_2_), channel_id=1, source_target_pairs={{0,16},{1,17},{2,18},{3,19},{4,20},{5,21},{6,22},{7,23},{8,24},{9,... | collective-permute-start | bytes 1032200 | tf_op jit(solution)/shard_map/ppermute | solution.py:23
  50.1 1.0 %collective-permute-done.13.refs_10_.refs_5_ = bf16[21,64,128]{2,1,0:T(8,128)(2,1)S(1)} collective-permute-done((bf16[21,64,128]{2,1,0:T(8,128)(2,1)S(1)}, bf16[21,64,128]{2,1,0:T(8,128)(2,1)S(1)}, u32[]{:S(2)}, u32[]{:S(2)}) %collective-permute-start.13) | collective-permute-done | bytes 344096 | tf_op jit(solution)/shard_map/ppermute | solution.py:23
  51.7 1.1 %collective-permute-start.15 = (bf16[21,64,128]{2,1,0:T(8,128)(2,1)S(1)}, bf16[21,64,128]{2,1,0:T(8,128)(2,1)S(1)}, u32[]{:S(2)}, u32[]{:S(2)}) collective-permute-start(bf16[21,64,128]{2,1,0:T(8,128)(2,1)S(1)} %get-tuple-element.75), channel_id=1, source_target_pairs={{0,2},{1,3},{2,0},{3,1},{4,6},{5,7},{6,4},{7,5},{8,10},{9,11},{10,... | collective-permute-start | bytes 1032200 | tf_op jit(solution)/shard_map/ppermute | solution.py:23
  53.4 3.0 %collective-permute-start.17 = (bf16[22,64,128]{2,1,0:T(8,128)(2,1)S(1)}, bf16[22,64,128]{2,1,0:T(8,128)(2,1)S(1)}, u32[]{:S(2)}, u32[]{:S(2)}) collective-permute-start(bf16[22,64,128]{2,1,0:T(8,128)(2,1)S(1)} %level1_1_1.1.refs_7_.refs_3_), channel_id=1, source_target_pairs={{0,16},{1,17},{2,18},{3,19},{4,20},{5,21},{6,22},{7,23},{8,24},{9,... | collective-permute-start | bytes 1081352 | tf_op jit(solution)/shard_map/ppermute | solution.py:23
  56.4 1.1 %early_0_0.1 = (bf16[64,64,128]{2,1,0:T(8,128)(2,1)S(1)}, bf16[43,64,128]{2,1,0:T(8,128)(2,1)S(1)}) custom-call(s32[8,64]{1,0:T(8,128)S(4)} %get-tuple-element.50.refs_0_, bf16[2,64,128,128]{3,2,1,0:T(8,128)(2,1)S(1)} %get-tuple-element.51.refs_7_.refs_8_.refs_1_.refs_10_.refs_9_.refs_6_.refs_5_, bf16[21,64,128]{2,1,0:T(8,128)(2,1)S(1)} %level1_0_0.1.refs_5_.refs_2_, ...), custom_call_target="tpu_custom_call" | custom-call | bytes 2000000 | tf_op jit(solution)/shard_map/early_0_0/pallas_call | solution.py:44
  57.6 1.4 %late_0_0.1 = (bf16[16,64,128]{2,1,0:T(8,128)(2,1)S(1)}, f32[16,64,128]{2,1,0:T(8,128)S(1)}, bf16[64,64,128]{2,1,0:T(8,128)(2,1)S(1)}) custom-call(s32[8,64]{1,0:T(8,128)S(4)} %get-tuple-element.50.refs_0_, bf16[2,64,128,128]{3,2,1,0:T(8,128)(2,1)S(1)} %get-tuple-element.51.refs_7_.refs_8_.refs_1_.refs_10_.refs_9_.refs_6_.refs_5_, ...), custom_call_target="tpu_custom_call" | custom-call | bytes 2000000 | tf_op jit(solution)/shard_map/late_0_0/pallas_call | solution.py:44
  59.9 1.9 %collective-permute-done.15.refs_2_ = bf16[21,64,128]{2,1,0:T(8,128)(2,1)S(1)} collective-permute-done((bf16[21,64,128]{2,1,0:T(8,128)(2,1)S(1)}, bf16[21,64,128]{2,1,0:T(8,128)(2,1)S(1)}, u32[]{:S(2)}, u32[]{:S(2)}) %collective-permute-start.15) | collective-permute-done | bytes 344096 | tf_op jit(solution)/shard_map/ppermute | solution.py:23
  62.4 3.0 %collective-permute-start.20 = (bf16[21,64,128]{2,1,0:T(8,128)(2,1)S(1)}, bf16[21,64,128]{2,1,0:T(8,128)(2,1)S(1)}, u32[]{:S(2)}, u32[]{:S(2)}) collective-permute-start(bf16[21,64,128]{2,1,0:T(8,128)(2,1)S(1)} %level1_1_2.1.refs_4_.refs_7_), channel_id=1, source_target_pairs={{0,16},{1,17},{2,18},{3,19},{4,20},{5,21},{6,22},{7,23},{8,24},{9,... | collective-permute-start | bytes 1032200 | tf_op jit(solution)/shard_map/ppermute | solution.py:23
  65.4 4.7 %collective-permute-start.14 = (bf16[16,64,128]{2,1,0:T(8,128)(2,1)S(1)}, bf16[16,64,128]{2,1,0:T(8,128)(2,1)S(1)}, u32[]{:S(2)}, u32[]{:S(2)}) collective-permute-start(bf16[16,64,128]{2,1,0:T(8,128)(2,1)S(1)} %get-tuple-element.74), channel_id=1, source_target_pairs={{0,32},{32,0},{64,96},{96,64},{1,33},{33,1},{65,97},{97,65},{2,34}... | collective-permute-start | bytes 786440 | tf_op jit(solution)/shard_map/ppermute | solution.py:23
  70.1 1.1 %early_1_0.1 = (bf16[64,64,128]{2,1,0:T(8,128)(2,1)S(1)}, bf16[43,64,128]{2,1,0:T(8,128)(2,1)S(1)}) custom-call(s32[8,64]{1,0:T(8,128)S(4)} %get-tuple-element.50.refs_0_, bf16[2,64,128,128]{3,2,1,0:T(8,128)(2,1)S(1)} %get-tuple-element.51.refs_7_.refs_8_.refs_1_.refs_10_.refs_9_.refs_6_.refs_5_, bf16[21,64,128]{2,1,0:T(8,128)(2,1)S(1)} %level1_1_0.1.refs_5_.refs_2_, ...), custom_call_target="tpu_custom_call" | custom-call | bytes 20000000 | tf_op jit(solution)/shard_map/early_1_0/pallas_call | solution.py:44
  71.3 1.1 %collective-permute-start.18 = (bf16[16,64,128]{2,1,0:T(8,128)(2,1)S(1)}, bf16[16,64,128]{2,1,0:T(8,128)(2,1)S(1)}, u32[]{:S(2)}, u32[]{:S(2)}) collective-permute-start(bf16[16,64,128]{2,1,0:T(8,128)(2,1)S(1)} %join_0_0.1.refs_6_), channel_id=1, source_target_pairs={{0,64},{32,96},{64,0},{96,32},{1,65},{33,97},{65,1},{97,33},{2,66}... | collective-permute-start | bytes 786440 | tf_op jit(solution)/shard_map/ppermute | solution.py:23
  72.4 1.8 %collective-permute-done.20.refs_5_ = bf16[21,64,128]{2,1,0:T(8,128)(2,1)S(1)} collective-permute-done((bf16[21,64,128]{2,1,0:T(8,128)(2,1)S(1)}, bf16[21,64,128]{2,1,0:T(8,128)(2,1)S(1)}, u32[]{:S(2)}, u32[]{:S(2)}) %collective-permute-start.20) | collective-permute-done | bytes 344096 | tf_op jit(solution)/shard_map/ppermute | solution.py:23
  74.1 1.4 %late_1_0.1 = (bf16[16,64,128]{2,1,0:T(8,128)(2,1)S(1)}, f32[16,64,128]{2,1,0:T(8,128)S(1)}, bf16[64,64,128]{2,1,0:T(8,128)(2,1)S(1)}) custom-call(s32[8,64]{1,0:T(8,128)S(4)} %get-tuple-element.50.refs_0_, bf16[2,64,128,128]{3,2,1,0:T(8,128)(2,1)S(1)} %get-tuple-element.51.refs_7_.refs_8_.refs_1_.refs_10_.refs_9_.refs_6_.refs_5_, ...), custom_call_target="tpu_custom_call" | custom-call | bytes 2000000 | tf_op jit(solution)/shard_map/late_1_0/pallas_call | solution.py:44
  75.6 4.4 %collective-permute-start.21 = (bf16[16,64,128]{2,1,0:T(8,128)(2,1)S(1)}, bf16[16,64,128]{2,1,0:T(8,128)(2,1)S(1)}, u32[]{:S(2)}, u32[]{:S(2)}) collective-permute-start(bf16[16,64,128]{2,1,0:T(8,128)(2,1)S(1)} %get-tuple-element.82), channel_id=1, source_target_pairs={{0,32},{32,0},{64,96},{96,64},{1,33},{33,1},{65,97},{97,65},{2,34}... | collective-permute-start | bytes 786440 | tf_op jit(solution)/shard_map/ppermute | solution.py:23
  80.0 1.2 %collective-permute-done.21.refs_1_ = bf16[16,64,128]{2,1,0:T(8,128)(2,1)S(1)} collective-permute-done((bf16[16,64,128]{2,1,0:T(8,128)(2,1)S(1)}, bf16[16,64,128]{2,1,0:T(8,128)(2,1)S(1)}, u32[]{:S(2)}, u32[]{:S(2)}) %collective-permute-start.21) | collective-permute-done | bytes 262176 | tf_op jit(solution)/shard_map/ppermute | solution.py:23
  82.9 1.5 %collective-permute-start.23 = (bf16[8,64,128]{2,1,0:T(8,128)(2,1)S(1)}, bf16[8,64,128]{2,1,0:T(8,128)(2,1)S(1)}, u32[]{:S(2)}, u32[]{:S(2)}) collective-permute-start(bf16[8,64,128]{2,1,0:T(8,128)(2,1)S(1)} %get-tuple-element.85), channel_id=1, source_target_pairs={{0,32},{32,0},{64,96},{96,64},{1,33},{33,1},{65,97},{97,65},{2,34}... | collective-permute-start | bytes 393224 | tf_op jit(solution)/shard_map/ppermute | solution.py:23
  85.8 1.9 %collective-permute-done.22.refs_3_ = bf16[16,64,128]{2,1,0:T(8,128)(2,1)S(1)} collective-permute-done((bf16[16,64,128]{2,1,0:T(8,128)(2,1)S(1)}, bf16[16,64,128]{2,1,0:T(8,128)(2,1)S(1)}, u32[]{:S(2)}, u32[]{:S(2)}) %collective-permute-start.22) | collective-permute-done | bytes 262176 | tf_op jit(solution)/shard_map/ppermute | solution.py:23
  (42 shorter events, 14.7 us)
Async XLA Ops:
  1.6 12.6 %collective-permute-start = (bf16[22,64,128]{2,1,0:T(8,128)(2,1)S(1)}, bf16[22,64,128]{2,1,0:T(8,128)(2,1)S(1)}, u32[]{:S(2)}, u32[]{:S(2)}) collective-permute-start(bf16[22,64,128]{2,1,0:T(8,128)(2,1)S(1)} %get-tuple-element.53), channel_id=1, source_target_pairs={{0,1},{1,0},{2,3},{3,2},{4,5},{5,4},{6,7},{7,6},{8,9},{9,8},{10,11... | collective-permute-start | bytes 1081352 | tf_op jit(solution)/shard_map/ppermute | solution.py:23
  8.4 13.6 %collective-permute-start.2 = (bf16[22,64,128]{2,1,0:T(8,128)(2,1)S(1)}, bf16[22,64,128]{2,1,0:T(8,128)(2,1)S(1)}, u32[]{:S(2)}, u32[]{:S(2)}) collective-permute-start(bf16[22,64,128]{2,1,0:T(8,128)(2,1)S(1)} %get-tuple-element.57), channel_id=1, source_target_pairs={{0,1},{1,0},{2,3},{3,2},{4,5},{5,4},{6,7},{7,6},{8,9},{9,8},{10,11... | collective-permute-start | bytes 1081352 | tf_op jit(solution)/shard_map/ppermute | solution.py:23
  14.9 11.7 %collective-permute-start.1 = (bf16[21,64,128]{2,1,0:T(8,128)(2,1)S(1)}, bf16[21,64,128]{2,1,0:T(8,128)(2,1)S(1)}, u32[]{:S(2)}, u32[]{:S(2)}) collective-permute-start(bf16[21,64,128]{2,1,0:T(8,128)(2,1)S(1)} %get-tuple-element.56), channel_id=1, source_target_pairs={{0,2},{1,3},{2,0},{3,1},{4,6},{5,7},{6,4},{7,5},{8,10},{9,11},{10,... | collective-permute-start | bytes 1032200 | tf_op jit(solution)/shard_map/ppermute | solution.py:23
  16.3 13.8 %collective-permute-start.4 = (bf16[20,64,128]{2,1,0:T(8,128)(2,1)S(1)}, bf16[20,64,128]{2,1,0:T(8,128)(2,1)S(1)}, u32[]{:S(2)}, u32[]{:S(2)}) collective-permute-start(bf16[20,64,128]{2,1,0:T(8,128)(2,1)S(1)} %get-tuple-element.60), channel_id=1, source_target_pairs={{0,1},{1,0},{2,3},{3,2},{4,5},{5,4},{6,7},{7,6},{8,9},{9,8},{10,11... | collective-permute-start | bytes 983048 | tf_op jit(solution)/shard_map/ppermute | solution.py:23
  22.7 11.0 %collective-permute-start.3 = (bf16[22,64,128]{2,1,0:T(8,128)(2,1)S(1)}, bf16[22,64,128]{2,1,0:T(8,128)(2,1)S(1)}, u32[]{:S(2)}, u32[]{:S(2)}) collective-permute-start(bf16[22,64,128]{2,1,0:T(8,128)(2,1)S(1)} %get-tuple-element.59), channel_id=1, source_target_pairs={{0,2},{1,3},{2,0},{3,1},{4,6},{5,7},{6,4},{7,5},{8,10},{9,11},{10,... | collective-permute-start | bytes 1081352 | tf_op jit(solution)/shard_map/ppermute | solution.py:23
  24.0 13.1 %collective-permute-start.6 = (bf16[22,64,128]{2,1,0:T(8,128)(2,1)S(1)}, bf16[22,64,128]{2,1,0:T(8,128)(2,1)S(1)}, u32[]{:S(2)}, u32[]{:S(2)}) collective-permute-start(bf16[22,64,128]{2,1,0:T(8,128)(2,1)S(1)} %get-tuple-element.63), channel_id=1, source_target_pairs={{0,1},{1,0},{2,3},{3,2},{4,5},{5,4},{6,7},{7,6},{8,9},{9,8},{10,11... | collective-permute-start | bytes 1081352 | tf_op jit(solution)/shard_map/ppermute | solution.py:23
  27.3 9.8 %collective-permute-start.7 = (bf16[21,64,128]{2,1,0:T(8,128)(2,1)S(1)}, bf16[21,64,128]{2,1,0:T(8,128)(2,1)S(1)}, u32[]{:S(2)}, u32[]{:S(2)}) collective-permute-start(bf16[21,64,128]{2,1,0:T(8,128)(2,1)S(1)} %level1_0_0.1.refs_5_.refs_2_), channel_id=1, source_target_pairs={{0,16},{1,17},{2,18},{3,19},{4,20},{5,21},{6,22},{7,23},{8,24},{9,... | collective-permute-start | bytes 1032200 | tf_op jit(solution)/shard_map/ppermute | solution.py:23
  30.7 8.1 %collective-permute-start.5 = (bf16[21,64,128]{2,1,0:T(8,128)(2,1)S(1)}, bf16[21,64,128]{2,1,0:T(8,128)(2,1)S(1)}, u32[]{:S(2)}, u32[]{:S(2)}) collective-permute-start(bf16[21,64,128]{2,1,0:T(8,128)(2,1)S(1)} %get-tuple-element.62), channel_id=1, source_target_pairs={{0,2},{1,3},{2,0},{3,1},{4,6},{5,7},{6,4},{7,5},{8,10},{9,11},{10,... | collective-permute-start | bytes 1032200 | tf_op jit(solution)/shard_map/ppermute | solution.py:23
  31.0 13.8 %collective-permute-start.9 = (bf16[22,64,128]{2,1,0:T(8,128)(2,1)S(1)}, bf16[22,64,128]{2,1,0:T(8,128)(2,1)S(1)}, u32[]{:S(2)}, u32[]{:S(2)}) collective-permute-start(bf16[22,64,128]{2,1,0:T(8,128)(2,1)S(1)} %get-tuple-element.65), channel_id=1, source_target_pairs={{0,1},{1,0},{2,3},{3,2},{4,5},{5,4},{6,7},{7,6},{8,9},{9,8},{10,11... | collective-permute-start | bytes 1081352 | tf_op jit(solution)/shard_map/ppermute | solution.py:23
  34.3 10.6 %collective-permute-start.8 = (bf16[22,64,128]{2,1,0:T(8,128)(2,1)S(1)}, bf16[22,64,128]{2,1,0:T(8,128)(2,1)S(1)}, u32[]{:S(2)}, u32[]{:S(2)}) collective-permute-start(bf16[22,64,128]{2,1,0:T(8,128)(2,1)S(1)} %level1_0_1.1.refs_4_.refs_3_), channel_id=1, source_target_pairs={{0,16},{1,17},{2,18},{3,19},{4,20},{5,21},{6,22},{7,23},{8,24},{9,... | collective-permute-start | bytes 1081352 | tf_op jit(solution)/shard_map/ppermute | solution.py:23
  37.8 8.4 %collective-permute-start.12 = (bf16[21,64,128]{2,1,0:T(8,128)(2,1)S(1)}, bf16[21,64,128]{2,1,0:T(8,128)(2,1)S(1)}, u32[]{:S(2)}, u32[]{:S(2)}) collective-permute-start(bf16[21,64,128]{2,1,0:T(8,128)(2,1)S(1)} %get-tuple-element.69), channel_id=1, source_target_pairs={{0,2},{1,3},{2,0},{3,1},{4,6},{5,7},{6,4},{7,5},{8,10},{9,11},{10,... | collective-permute-start | bytes 1032200 | tf_op jit(solution)/shard_map/ppermute | solution.py:23
  39.4 11.7 %collective-permute-start.13 = (bf16[21,64,128]{2,1,0:T(8,128)(2,1)S(1)}, bf16[21,64,128]{2,1,0:T(8,128)(2,1)S(1)}, u32[]{:S(2)}, u32[]{:S(2)}) collective-permute-start(bf16[21,64,128]{2,1,0:T(8,128)(2,1)S(1)} %level1_0_2.1.refs_5_.refs_4_), channel_id=1, source_target_pairs={{0,16},{1,17},{2,18},{3,19},{4,20},{5,21},{6,22},{7,23},{8,24},{9,... | collective-permute-start | bytes 1032200 | tf_op jit(solution)/shard_map/ppermute | solution.py:23
  42.2 7.9 %collective-permute-start.11 = (bf16[20,64,128]{2,1,0:T(8,128)(2,1)S(1)}, bf16[20,64,128]{2,1,0:T(8,128)(2,1)S(1)}, u32[]{:S(2)}, u32[]{:S(2)}) collective-permute-start(bf16[20,64,128]{2,1,0:T(8,128)(2,1)S(1)} %get-tuple-element.68), channel_id=1, source_target_pairs={{0,1},{1,0},{2,3},{3,2},{4,5},{5,4},{6,7},{7,6},{8,9},{9,8},{10,11... | collective-permute-start | bytes 983048 | tf_op jit(solution)/shard_map/ppermute | solution.py:23
  45.5 7.3 %collective-permute-start.10 = (bf16[22,64,128]{2,1,0:T(8,128)(2,1)S(1)}, bf16[22,64,128]{2,1,0:T(8,128)(2,1)S(1)}, u32[]{:S(2)}, u32[]{:S(2)}) collective-permute-start(bf16[22,64,128]{2,1,0:T(8,128)(2,1)S(1)} %get-tuple-element.67), channel_id=1, source_target_pairs={{0,2},{1,3},{2,0},{3,1},{4,6},{5,7},{6,4},{7,5},{8,10},{9,11},{10,... | collective-permute-start | bytes 1081352 | tf_op jit(solution)/shard_map/ppermute | solution.py:23
  46.8 12.3 %collective-permute-start.16 = (bf16[21,64,128]{2,1,0:T(8,128)(2,1)S(1)}, bf16[21,64,128]{2,1,0:T(8,128)(2,1)S(1)}, u32[]{:S(2)}, u32[]{:S(2)}) collective-permute-start(bf16[21,64,128]{2,1,0:T(8,128)(2,1)S(1)} %level1_1_0.1.refs_5_.refs_2_), channel_id=1, source_target_pairs={{0,16},{1,17},{2,18},{3,19},{4,20},{5,21},{6,22},{7,23},{8,24},{9,... | collective-permute-start | bytes 1032200 | tf_op jit(solution)/shard_map/ppermute | solution.py:23
  51.7 10.1 %collective-permute-start.15 = (bf16[21,64,128]{2,1,0:T(8,128)(2,1)S(1)}, bf16[21,64,128]{2,1,0:T(8,128)(2,1)S(1)}, u32[]{:S(2)}, u32[]{:S(2)}) collective-permute-start(bf16[21,64,128]{2,1,0:T(8,128)(2,1)S(1)} %get-tuple-element.75), channel_id=1, source_target_pairs={{0,2},{1,3},{2,0},{3,1},{4,6},{5,7},{6,4},{7,5},{8,10},{9,11},{10,... | collective-permute-start | bytes 1032200 | tf_op jit(solution)/shard_map/ppermute | solution.py:23
  53.4 16.7 %collective-permute-start.17 = (bf16[22,64,128]{2,1,0:T(8,128)(2,1)S(1)}, bf16[22,64,128]{2,1,0:T(8,128)(2,1)S(1)}, u32[]{:S(2)}, u32[]{:S(2)}) collective-permute-start(bf16[22,64,128]{2,1,0:T(8,128)(2,1)S(1)} %level1_1_1.1.refs_7_.refs_3_), channel_id=1, source_target_pairs={{0,16},{1,17},{2,18},{3,19},{4,20},{5,21},{6,22},{7,23},{8,24},{9,... | collective-permute-start | bytes 1081352 | tf_op jit(solution)/shard_map/ppermute | solution.py:23
  62.4 11.8 %collective-permute-start.20 = (bf16[21,64,128]{2,1,0:T(8,128)(2,1)S(1)}, bf16[21,64,128]{2,1,0:T(8,128)(2,1)S(1)}, u32[]{:S(2)}, u32[]{:S(2)}) collective-permute-start(bf16[21,64,128]{2,1,0:T(8,128)(2,1)S(1)} %level1_1_2.1.refs_4_.refs_7_), channel_id=1, source_target_pairs={{0,16},{1,17},{2,18},{3,19},{4,20},{5,21},{6,22},{7,23},{8,24},{9,... | collective-permute-start | bytes 1032200 | tf_op jit(solution)/shard_map/ppermute | solution.py:23
  65.4 5.9 %collective-permute-start.14 = (bf16[16,64,128]{2,1,0:T(8,128)(2,1)S(1)}, bf16[16,64,128]{2,1,0:T(8,128)(2,1)S(1)}, u32[]{:S(2)}, u32[]{:S(2)}) collective-permute-start(bf16[16,64,128]{2,1,0:T(8,128)(2,1)S(1)} %get-tuple-element.74), channel_id=1, source_target_pairs={{0,32},{32,0},{64,96},{96,64},{1,33},{33,1},{65,97},{97,65},{2,34}... | collective-permute-start | bytes 786440 | tf_op jit(solution)/shard_map/ppermute | solution.py:23
  70.1 2.3 %collective-permute-start.19 = (bf16[16,64,128]{2,1,0:T(8,128)(2,1)S(1)}, bf16[16,64,128]{2,1,0:T(8,128)(2,1)S(1)}, u32[]{:S(2)}, u32[]{:S(2)}) collective-permute-start(bf16[16,64,128]{2,1,0:T(8,128)(2,1)S(1)} %get-tuple-element.79), channel_id=1, source_target_pairs={{0,32},{32,0},{64,96},{96,64},{1,33},{33,1},{65,97},{97,65},{2,34}... | collective-permute-start | bytes 786440 | tf_op jit(solution)/shard_map/ppermute | solution.py:23
  71.3 8.7 %collective-permute-start.18 = (bf16[16,64,128]{2,1,0:T(8,128)(2,1)S(1)}, bf16[16,64,128]{2,1,0:T(8,128)(2,1)S(1)}, u32[]{:S(2)}, u32[]{:S(2)}) collective-permute-start(bf16[16,64,128]{2,1,0:T(8,128)(2,1)S(1)} %join_0_0.1.refs_6_), channel_id=1, source_target_pairs={{0,64},{32,96},{64,0},{96,32},{1,65},{33,97},{65,1},{97,33},{2,66}... | collective-permute-start | bytes 786440 | tf_op jit(solution)/shard_map/ppermute | solution.py:23
  75.6 5.5 %collective-permute-start.21 = (bf16[16,64,128]{2,1,0:T(8,128)(2,1)S(1)}, bf16[16,64,128]{2,1,0:T(8,128)(2,1)S(1)}, u32[]{:S(2)}, u32[]{:S(2)}) collective-permute-start(bf16[16,64,128]{2,1,0:T(8,128)(2,1)S(1)} %get-tuple-element.82), channel_id=1, source_target_pairs={{0,32},{32,0},{64,96},{96,64},{1,33},{33,1},{65,97},{97,65},{2,34}... | collective-permute-start | bytes 786440 | tf_op jit(solution)/shard_map/ppermute | solution.py:23
  81.2 6.6 %collective-permute-start.22 = (bf16[16,64,128]{2,1,0:T(8,128)(2,1)S(1)}, bf16[16,64,128]{2,1,0:T(8,128)(2,1)S(1)}, u32[]{:S(2)}, u32[]{:S(2)}) collective-permute-start(bf16[16,64,128]{2,1,0:T(8,128)(2,1)S(1)} %join_1_0.1.refs_3_), channel_id=1, source_target_pairs={{0,64},{32,96},{64,0},{96,32},{1,65},{33,97},{65,1},{97,33},{2,66}... | collective-permute-start | bytes 786440 | tf_op jit(solution)/shard_map/ppermute | solution.py:23
  82.9 2.5 %collective-permute-start.23 = (bf16[8,64,128]{2,1,0:T(8,128)(2,1)S(1)}, bf16[8,64,128]{2,1,0:T(8,128)(2,1)S(1)}, u32[]{:S(2)}, u32[]{:S(2)}) collective-permute-start(bf16[8,64,128]{2,1,0:T(8,128)(2,1)S(1)} %get-tuple-element.85), channel_id=1, source_target_pairs={{0,32},{32,0},{64,96},{96,64},{1,33},{33,1},{65,97},{97,65},{2,34}... | collective-permute-start | bytes 393224 | tf_op jit(solution)/shard_map/ppermute | solution.py:23
  84.5 1.3 %collective-permute-start.24 = (bf16[8,64,128]{2,1,0:T(8,128)(2,1)S(1)}, bf16[8,64,128]{2,1,0:T(8,128)(2,1)S(1)}, u32[]{:S(2)}, u32[]{:S(2)}) collective-permute-start(bf16[8,64,128]{2,1,0:T(8,128)(2,1)S(1)} %get-tuple-element.86), channel_id=1, source_target_pairs={{0,32},{32,0},{64,96},{96,64},{1,33},{33,1},{65,97},{97,65},{2,34}... | collective-permute-start | bytes 393224 | tf_op jit(solution)/shard_map/ppermute | solution.py:23

commit v3 on v2

--- a/solution.py
+++ b/solution.py
@@ -31,7 +31,7 @@
     return jnp.concatenate([a, b], axis=1)
 
 
-def call(kernel, name, outs, ins, specs, dep, scratch=(), mb=4, out_specs=None, cost=2000000):
+def call(kernel, name, outs, ins, specs, dep, scratch=(), mb=4, out_specs=None, cost=2000000, aliases=None):
     outs = tuple(outs)
     extra = tuple(dep)
 
@@ -50,6 +50,7 @@
         compiler_params=pltpu.CompilerParams(vmem_limit_bytes=mb << 20),
         cost_estimate=pl.CostEstimate(flops=0, bytes_accessed=cost, transcendentals=0),
         name=name,
+        input_output_aliases=aliases or {},
     )(*ins, *extra)
 
 
@@ -68,7 +69,6 @@
 
 
 def pad(out, used):
-    return
     for i in range(used, out.shape[0]):
         out[i] = jnp.zeros(out.shape[1:], out.dtype)
 
@@ -240,7 +240,13 @@
             ref[i % out[0].shape[0]] = total.astype(ref.dtype)
 
 
-def late_kernel(piece, order, w, w3, x2, x3, got, send, keep, full):
+def place():
+    me = lax.axis_index("hi")
+    return me // 2, me % 2
+
+
+def late_kernel(piece, order, w, w3, x2, x3, got, *outs):
+    send, keep, full = outs if len(outs) == 3 else (outs[0], None, outs[1])
     _, _, sizes = PIECES[piece]
     edge, _ = bounds(sizes)
     last = edge[-2]
@@ -249,15 +255,20 @@
     for i in range(sizes[-1]):
         j = order[TJ, last + i]
         full[j] = mm(cat(x2[order[POS, j]], got[i]), factors(w, j)).astype(BF)
-    me = lax.axis_index("hi")
-    z, core = me // 2, me % 2
-    products(order, w3, full, (2 * (1 - z) + 1 - core, 2 * (1 - z) + core), ([send], [keep]))
+    z, core = place()
+    products(order, w3, full, [2 * (1 - z) + 1 - core], ([send],))
+    if keep is not None:
+        products(order, w3, full, [2 * (1 - z) + core], ([keep],))
+
+
+def keep_kernel(order, w3, full, keep):
+    z, core = place()
+    products(order, w3, full, [2 * (1 - z) + core], ([keep],))
 
 
 def rest_kernel(order, w3, full, *outs):
     *sends, keep = outs
-    me = lax.axis_index("hi")
-    z, core = me // 2, me % 2
+    z, core = place()
     products(order, w3, full, (2 * z + 1 - core, 2 * z + core), (sends, [keep]))
 
 
@@ -265,17 +276,23 @@
     send[...] = (keep[...] + got[...].astype(F32)).astype(BF)
 
 
-def final_kernel(*refs):
-    refs, out = list(refs[:-1]), refs[-1]
-    for piece, (r0, rows, _) in enumerate(PIECES):
-        far, own, *cores = refs[: 3 + piece]
-        del refs[: 3 + piece]
-        base = 0
-        for core in cores:
-            part = pl.ds(base, core.shape[0])
-            base += core.shape[0]
-            total = own[part] + core[...].astype(F32) + far[part].astype(F32)
-            out[part, pl.ds(r0, rows), :] = total.astype(BF)
+def final_kernel(piece, *refs):
+    r0, rows, _ = PIECES[piece]
+    refs = list(refs)
+    far, own, *cores = refs[: 3 + piece]
+    out, stage, sem = refs[-3:]
+    base, copies = 0, []
+    for i, core in enumerate(cores):
+        part = pl.ds(base, core.shape[0])
+        base += core.shape[0]
+        total = own[part] + core[...].astype(F32) + far[part].astype(F32)
+        stage[part] = total.astype(BF)
+        copies.append(
+            pltpu.make_async_copy(stage.at[part], out.at[part, pl.ds(r0, rows), :], sem.at[i])
+        )
+        copies[-1].start()
+    for copy in copies:
+        copy.wait()
 
 
 def plan():
@@ -287,8 +304,9 @@
         if s:
             steps.append(("level1", *chunks[s - 1]))
     last = steps.pop()
-    steps += [last, ("early", 0, 0), ("late", 0, 0), ("rest", 0, 0), ("level1", *chunks[-1])]
+    steps += [("early", 0, 0), last, ("late", 0, 0), ("rest", 0, 0), ("level1", *chunks[-1])]
     steps += [("early", 1, 0), ("join", 0, 0), ("late", 1, 0), ("join", 1, 0), ("rest", 1, 0)]
+    steps += [("final", 0, 0), ("final", 1, 0)]
     return chunks, steps
 
 
@@ -299,7 +317,8 @@
 
     def zshape(piece, k):
         _, zed = bounds(PIECES[piece][2])
-        return pltpu.VMEM((zed[k + 1] - zed[k], PIECES[piece][1], P_), BF)
+        size = zed[k + 1] - zed[k] if (piece, k) == chunks[-1] else slots(piece)
+        return pltpu.VMEM((size, PIECES[piece][1], P_), BF)
 
     first = chunks[: DEPTH + 1]
     wshape = pltpu.VMEM((2, NB, P_, P_), BF)
@@ -347,10 +366,10 @@
         part = lambda count, dtype: pltpu.VMEM((count, rows, P_), dtype)
         if kind == "level0":
             s = chunks.index(c)
-            if s > 2:
+            if 2 < s < len(chunks) - 1:
                 dep = (*dep, xin[chunks[s - 3]])
             after = chunks[s + DEPTH] if 0 < s < len(chunks) - DEPTH else None
-            outs = [part(sizes[k] + 2, BF), part(sizes[k], BF)]
+            outs = [part(sizes[k] + 2, BF), part(sizes[k] if c == chunks[-1] else slots(piece), BF)]
             outs += [zshape(*after)] if after else []
             ins = [order, x0, zin[c], w[0]] + ([xs[piece, k - 1]] if k else [])
             specs = [SM] + [VM] * (len(ins) - 1)
@@ -365,13 +384,15 @@
         elif kind == "level1":
             (x2[c],) = call(
                 functools.partial(level1_kernel, piece, k),
-                name, [part(sizes[k], BF)],
+                name, [part(sizes[k] if c == chunks[-1] else slots(piece), BF)],
                 [order, xs[c], yin[c], w[1]], [SM, VM, VM, VM], dep,
             )
             xin[c] = partner_2(x2[c], "lo", top - 1)
             dep = x2[c]
         elif kind == "early":
             n = len(sizes)
+            if not piece:
+                dep = (*dep, xin[chunks[-4]])
             ins = [order, w[2]] + [x2[piece, i] for i in range(n)] + [xin[piece, i] for i in range(n - 1)]
             early[piece] = call(
                 functools.partial(early_kernel, piece),
@@ -382,14 +403,21 @@
         elif kind == "late":
             if piece:
                 dep = (*dep, *chip[piece - 1][1:])
-            send, keep, full = call(
+            outs = [part(NB // 4, BF), part(NB, BF)]
+            send, *keep, full = call(
                 functools.partial(late_kernel, piece),
-                name, [part(NB // 4, BF), part(NB // 4, F32), part(NB, BF)],
+                name, outs if piece else [outs[0], part(NB // 4, F32), outs[1]],
                 [order, w[2], w[3], *early[piece], xin[piece, len(sizes) - 1]], [SM] + [VM] * 5, dep,
             )
             late[piece] = full
-            core[piece] = keep, partner_2(send, "hi", 0)
-            dep = keep
+            got = partner_2(send, "hi", 0)
+            dep = send
+            if piece:
+                keep = call(
+                    keep_kernel, "keep", [part(NB // 4, F32)], [order, w[3], full], [SM, VM, VM], (dep, *w),
+                )
+                dep = keep[0]
+            core[piece] = keep[0], got
         elif kind == "rest":
             if not piece:
                 dep = (*dep, xin[chunks[-3]])
@@ -401,17 +429,22 @@
             )
             chip[piece] = keep, *[partner_2(send, "hi", 0) for send in sends]
             dep = keep
+        elif kind == "final":
+            ins = [far[piece], *chip[piece]] + ([out] if piece else [])
+            (out,) = call(
+                functools.partial(final_kernel, piece),
+                name, [jax.ShapeDtypeStruct((NB // 4, P_, P_), BF)],
+                ins, [VM] * (2 + 1 + piece) + ([ANY] if piece else []), () if piece else dep,
+                scratch=[pltpu.VMEM((NB // 4, rows, P_), BF), pltpu.SemaphoreType.DMA((2,))],
+                out_specs=[ANY], aliases={len(ins) - 1: 0} if piece else None,
+            )
+            dep = out
         else:
             if piece:
                 dep = (*dep, far[piece - 1])
             (send,) = call(join_kernel, name, [part(NB // 4, BF)], [*core[piece]], [VM, VM], dep)
             far[piece] = partner_2(send, "hi", 1)
             dep = send
-    ins = [a for piece in range(len(PIECES)) for a in (far[piece], *chip[piece])]
-    (out,) = call(
-        final_kernel, "final", [jax.ShapeDtypeStruct((NB // 4, P_, P_), BF)],
-        ins, [VM] * len(ins), (),
-    )
     return out
 
 

time: 89.7 us -> 89 us (level)
  starting transfers between devices: 51.3 us -> 48.6 us
  waiting for transfers between devices: 13.4 us -> 15.3 us
    ppermute x25, starting transfers between devices: 51.3 us -> 48.6 us  [partner_2(): lax.ppermute(array, axis, [(i, i ^ 1 << apart) for i in range(lax.axis_si...]
    ppermute x25, waiting for transfers between devices: 13.4 us -> 15.3 us  [partner_2(): lax.ppermute(array, axis, [(i, i ^ 1 << apart) for i in range(lax.axis_si...]
    pallas_call x24 -> x26, Pallas kernels: 23.9 us -> 24.6 us  [call(): pl.pallas_call(run, out_shape=outs, in_specs=list(specs) + [ANY] * len(ex...]
  transfers between devices with their start and end apart: 25 -> 25, of which waited for: 10 -> 9; matrix products, arithmetic and copies ran while one was open for 0% -> 0% of each run, Pallas kernels for 24% -> 25%
where the time goes in v3:
time: 89 us; the launch traced here: 88.8 us
  starting transfers between devices  48.6 us (55%)
  Pallas kernels  24.6 us (28%)
  waiting for transfers between devices  15.3 us (17%)
    ppermute x25, starting transfers between devices, partner_2(): lax.ppermute(array, axis, [(i, i ^ 1 << apart) for i in range(lax.axis_si...  48.6 us
    pallas_call x26, Pallas kernels, call(): pl.pallas_call(run, out_shape=outs, in_specs=list(specs) + [ANY] * len(ex...  24.6 us
    ppermute x25, waiting for transfers between devices, partner_2(): lax.ppermute(array, axis, [(i, i ^ 1 << apart) for i in range(lax.axis_si...  15.3 us
  transfers between devices with their start and end apart: 25, of which 9 were waited for; matrix products, arithmetic and copies ran while one was open for 0% of the time, Pallas kernels for 25%

profile of v3, /device:TPU:1, one launch (start us, length us, event | category | flops | bytes accessed | tf_op | source)
XLA Modules:
  0.0 88.8 jit_solution(15395352135207859935)
XLA Ops:
  0.0 1.6 %head.1 = (s32[4,64]{1,0:T(4,128)S(4)}, bf16[64,128,128]{2,1,0:T(8,128)(2,1)S(1)}, bf16[22,64,128]{2,1,0:T(8,128)(2,1)S(1)}) custom-call(s32[4,64]{1,0:T(4,128)} %refs_0_.1, bf16[64,128,128]{2,1,0:T(8,128)(2,1)} %refs_1_.1), custom_call_target="tpu_custom_call" | custom-call | bytes 2000000 | tf_op jit(solution)/shard_map/head/pallas_call | solution.py:44
  1.6 4.5 %collective-permute-start.1 = (bf16[22,64,128]{2,1,0:T(8,128)(2,1)S(1)}, bf16[22,64,128]{2,1,0:T(8,128)(2,1)S(1)}, u32[]{:S(2)}, u32[]{:S(2)}) collective-permute-start(bf16[22,64,128]{2,1,0:T(8,128)(2,1)S(1)} %get-tuple-element.53), channel_id=1, source_target_pairs={{0,1},{1,0},{2,3},{3,2},{4,5},{5,4},{6,7},{7,6},{8,9},{9,8},{10,11... | collective-permute-start | bytes 1081352 | tf_op jit(solution)/shard_map/ppermute | solution.py:23
  6.1 2.2 %next.1 = (s32[3,64]{1,0:T(4,128)S(4)}, bf16[2,64,128,128]{3,2,1,0:T(8,128)(2,1)S(1)}, bf16[22,64,128]{2,1,0:T(8,128)(2,1)S(1)}, bf16[22,64,128]{2,1,0:T(8,128)(2,1)S(1)}) custom-call(s32[4,64]{1,0:T(4,128)S(4)} %get-tuple-element.45.refs_0_, bf16[64,128,128]{2,1,0:T(8,128)(2,1)S(1)} %get-tuple-element.46.refs_1_.refs_4_, bf16[4,64,128,128]{3,2,1,0:T(8,128)(2,1)} %refs_2_.3, ...), custom_call_target="tpu_custom_call" | custom-call | bytes 2000000 | tf_op jit(solution)/shard_map/next/pallas_call | solution.py:44
  8.5 4.7 %tables.1 = (s32[8,64]{1,0:T(8,128)S(4)}, bf16[2,64,128,128]{3,2,1,0:T(8,128)(2,1)S(1)}, bf16[2,64,128,128]{3,2,1,0:T(8,128)(2,1)S(1)}, bf16[2,64,128,128]{3,2,1,0:T(8,128)(2,1)S(1)}) custom-call(s32[4,64]{1,0:T(4,128)S(4)} %get-tuple-element.45.refs_0_, s32[3,64]{1,0:T(4,128)S(4)} %get-tuple-element.47.refs_1_, bf16[4,64,128,128]{3,2,1,0:T(8,128)(2,1)} %refs_2_.3, ...), custom_call_target="tpu_custom_call" | custom-call | bytes 2000000 | tf_op jit(solution)/shard_map/tables/pallas_call | solution.py:44
  13.2 1.1 %collective-permute-done.1.refs_2_ = bf16[22,64,128]{2,1,0:T(8,128)(2,1)S(1)} collective-permute-done((bf16[22,64,128]{2,1,0:T(8,128)(2,1)S(1)}, bf16[22,64,128]{2,1,0:T(8,128)(2,1)S(1)}, u32[]{:S(2)}, u32[]{:S(2)}) %collective-permute-start.1) | collective-permute-done | bytes 360480 | tf_op jit(solution)/shard_map/ppermute | solution.py:23
  14.9 1.4 %collective-permute-start.5 = (bf16[22,64,128]{2,1,0:T(8,128)(2,1)S(1)}, bf16[22,64,128]{2,1,0:T(8,128)(2,1)S(1)}, u32[]{:S(2)}, u32[]{:S(2)}) collective-permute-start(bf16[22,64,128]{2,1,0:T(8,128)(2,1)S(1)} %get-tuple-element.60), channel_id=1, source_target_pairs={{0,2},{1,3},{2,0},{3,1},{4,6},{5,7},{6,4},{7,5},{8,10},{9,11},{10,... | collective-permute-start | bytes 1081352 | tf_op jit(solution)/shard_map/ppermute | solution.py:23
  16.3 2.6 %collective-permute-start.4 = (bf16[22,64,128]{2,1,0:T(8,128)(2,1)S(1)}, bf16[22,64,128]{2,1,0:T(8,128)(2,1)S(1)}, u32[]{:S(2)}, u32[]{:S(2)}) collective-permute-start(bf16[22,64,128]{2,1,0:T(8,128)(2,1)S(1)} %get-tuple-element.59), channel_id=1, source_target_pairs={{0,1},{1,0},{2,3},{3,2},{4,5},{5,4},{6,7},{7,6},{8,9},{9,8},{10,11... | collective-permute-start | bytes 1081352 | tf_op jit(solution)/shard_map/ppermute | solution.py:23
  19.0 3.1 %collective-permute-done.refs_2_ = bf16[22,64,128]{2,1,0:T(8,128)(2,1)S(1)} collective-permute-done((bf16[22,64,128]{2,1,0:T(8,128)(2,1)S(1)}, bf16[22,64,128]{2,1,0:T(8,128)(2,1)S(1)}, u32[]{:S(2)}, u32[]{:S(2)}) %collective-permute-start) | collective-permute-done | bytes 360480 | tf_op jit(solution)/shard_map/ppermute | solution.py:23
  22.7 1.4 %collective-permute-start.3 = (bf16[22,64,128]{2,1,0:T(8,128)(2,1)S(1)}, bf16[22,64,128]{2,1,0:T(8,128)(2,1)S(1)}, u32[]{:S(2)}, u32[]{:S(2)}) collective-permute-start(bf16[22,64,128]{2,1,0:T(8,128)(2,1)S(1)} %get-tuple-element.58), channel_id=1, source_target_pairs={{0,2},{1,3},{2,0},{3,1},{4,6},{5,7},{6,4},{7,5},{8,10},{9,11},{10,... | collective-permute-start | bytes 1081352 | tf_op jit(solution)/shard_map/ppermute | solution.py:23
  24.0 2.6 %collective-permute-start.2 = (bf16[22,64,128]{2,1,0:T(8,128)(2,1)S(1)}, bf16[22,64,128]{2,1,0:T(8,128)(2,1)S(1)}, u32[]{:S(2)}, u32[]{:S(2)}) collective-permute-start(bf16[22,64,128]{2,1,0:T(8,128)(2,1)S(1)} %get-tuple-element.56), channel_id=1, source_target_pairs={{0,1},{1,0},{2,3},{3,2},{4,5},{5,4},{6,7},{7,6},{8,9},{9,8},{10,11... | collective-permute-start | bytes 1081352 | tf_op jit(solution)/shard_map/ppermute | solution.py:23
  27.3 2.8 %collective-permute-start.6 = (bf16[22,64,128]{2,1,0:T(8,128)(2,1)S(1)}, bf16[22,64,128]{2,1,0:T(8,128)(2,1)S(1)}, u32[]{:S(2)}, u32[]{:S(2)}) collective-permute-start(bf16[22,64,128]{2,1,0:T(8,128)(2,1)S(1)} %level1_0_0.1.refs_5_.refs_2_), channel_id=1, source_target_pairs={{0,16},{1,17},{2,18},{3,19},{4,20},{5,21},{6,22},{7,23},{8,24},{9,... | collective-permute-start | bytes 1081352 | tf_op jit(solution)/shard_map/ppermute | solution.py:23
  30.7 1.0 %collective-permute-start.9 = (bf16[22,64,128]{2,1,0:T(8,128)(2,1)S(1)}, bf16[22,64,128]{2,1,0:T(8,128)(2,1)S(1)}, u32[]{:S(2)}, u32[]{:S(2)}) collective-permute-start(bf16[22,64,128]{2,1,0:T(8,128)(2,1)S(1)} %get-tuple-element.65), channel_id=1, source_target_pairs={{0,2},{1,3},{2,0},{3,1},{4,6},{5,7},{6,4},{7,5},{8,10},{9,11},{10,... | collective-permute-start | bytes 1081352 | tf_op jit(solution)/shard_map/ppermute | solution.py:23
  31.7 2.6 %collective-permute-start.8 = (bf16[22,64,128]{2,1,0:T(8,128)(2,1)S(1)}, bf16[22,64,128]{2,1,0:T(8,128)(2,1)S(1)}, u32[]{:S(2)}, u32[]{:S(2)}) collective-permute-start(bf16[22,64,128]{2,1,0:T(8,128)(2,1)S(1)} %get-tuple-element.64), channel_id=1, source_target_pairs={{0,1},{1,0},{2,3},{3,2},{4,5},{5,4},{6,7},{7,6},{8,9},{9,8},{10,11... | collective-permute-start | bytes 1081352 | tf_op jit(solution)/shard_map/ppermute | solution.py:23
  35.0 2.8 %collective-permute-start.10 = (bf16[22,64,128]{2,1,0:T(8,128)(2,1)S(1)}, bf16[22,64,128]{2,1,0:T(8,128)(2,1)S(1)}, u32[]{:S(2)}, u32[]{:S(2)}) collective-permute-start(bf16[22,64,128]{2,1,0:T(8,128)(2,1)S(1)} %level1_0_1.1.refs_4_.refs_3_), channel_id=1, source_target_pairs={{0,16},{1,17},{2,18},{3,19},{4,20},{5,21},{6,22},{7,23},{8,24},{9,... | collective-permute-start | bytes 1081352 | tf_op jit(solution)/shard_map/ppermute | solution.py:23
  38.5 1.0 %collective-permute-start.7 = (bf16[22,64,128]{2,1,0:T(8,128)(2,1)S(1)}, bf16[22,64,128]{2,1,0:T(8,128)(2,1)S(1)}, u32[]{:S(2)}, u32[]{:S(2)}) collective-permute-start(bf16[22,64,128]{2,1,0:T(8,128)(2,1)S(1)} %get-tuple-element.63), channel_id=1, source_target_pairs={{0,2},{1,3},{2,0},{3,1},{4,6},{5,7},{6,4},{7,5},{8,10},{9,11},{10,... | collective-permute-start | bytes 1081352 | tf_op jit(solution)/shard_map/ppermute | solution.py:23
  39.5 2.6 %collective-permute-start.12 = (bf16[20,64,128]{2,1,0:T(8,128)(2,1)S(1)}, bf16[20,64,128]{2,1,0:T(8,128)(2,1)S(1)}, u32[]{:S(2)}, u32[]{:S(2)}) collective-permute-start(bf16[20,64,128]{2,1,0:T(8,128)(2,1)S(1)} %get-tuple-element.68), channel_id=1, source_target_pairs={{0,1},{1,0},{2,3},{3,2},{4,5},{5,4},{6,7},{7,6},{8,9},{9,8},{10,11... | collective-permute-start | bytes 983048 | tf_op jit(solution)/shard_map/ppermute | solution.py:23
  42.7 2.8 %collective-permute-start.13 = (bf16[22,64,128]{2,1,0:T(8,128)(2,1)S(1)}, bf16[22,64,128]{2,1,0:T(8,128)(2,1)S(1)}, u32[]{:S(2)}, u32[]{:S(2)}) collective-permute-start(bf16[22,64,128]{2,1,0:T(8,128)(2,1)S(1)} %level1_0_2.1.refs_5_.refs_4_), channel_id=1, source_target_pairs={{0,16},{1,17},{2,18},{3,19},{4,20},{5,21},{6,22},{7,23},{8,24},{9,... | collective-permute-start | bytes 1081352 | tf_op jit(solution)/shard_map/ppermute | solution.py:23
  47.4 3.2 %collective-permute-start.15 = (bf16[22,64,128]{2,1,0:T(8,128)(2,1)S(1)}, bf16[22,64,128]{2,1,0:T(8,128)(2,1)S(1)}, u32[]{:S(2)}, u32[]{:S(2)}) collective-permute-start(bf16[22,64,128]{2,1,0:T(8,128)(2,1)S(1)} %level1_1_0.1.refs_5_.refs_2_), channel_id=1, source_target_pairs={{0,16},{1,17},{2,18},{3,19},{4,20},{5,21},{6,22},{7,23},{8,24},{9,... | collective-permute-start | bytes 1081352 | tf_op jit(solution)/shard_map/ppermute | solution.py:23
  50.6 1.2 %collective-permute-done.12.refs_2_ = bf16[20,64,128]{2,1,0:T(8,128)(2,1)S(1)} collective-permute-done((bf16[20,64,128]{2,1,0:T(8,128)(2,1)S(1)}, bf16[20,64,128]{2,1,0:T(8,128)(2,1)S(1)}, u32[]{:S(2)}, u32[]{:S(2)}) %collective-permute-start.12) | collective-permute-done | bytes 327712 | tf_op jit(solution)/shard_map/ppermute | solution.py:23
  52.4 1.4 %collective-permute-start.14 = (bf16[21,64,128]{2,1,0:T(8,128)(2,1)S(1)}, bf16[21,64,128]{2,1,0:T(8,128)(2,1)S(1)}, u32[]{:S(2)}, u32[]{:S(2)}) collective-permute-start(bf16[21,64,128]{2,1,0:T(8,128)(2,1)S(1)} %get-tuple-element.71), channel_id=1, source_target_pairs={{0,2},{1,3},{2,0},{3,1},{4,6},{5,7},{6,4},{7,5},{8,10},{9,11},{10,... | collective-permute-start | bytes 1032200 | tf_op jit(solution)/shard_map/ppermute | solution.py:23
  53.8 1.1 %early_0_0.1 = (bf16[64,64,128]{2,1,0:T(8,128)(2,1)S(1)}, bf16[43,64,128]{2,1,0:T(8,128)(2,1)S(1)}) custom-call(s32[8,64]{1,0:T(8,128)S(4)} %get-tuple-element.49.refs_0_, bf16[2,64,128,128]{3,2,1,0:T(8,128)(2,1)S(1)} %get-tuple-element.51.refs_7_.refs_8_.refs_1_.refs_10_.refs_9_.refs_6_.refs_5_, bf16[22,64,128]{2,1,0:T(8,128)(2,1)S(1)} %level1_0_0.1.refs_5_.refs_2_, ...), custom_call_target="tpu_custom_call" | custom-call | bytes 2000000 | tf_op jit(solution)/shard_map/early_0_0/pallas_call | solution.py:44
  55.6 3.2 %collective-permute-start.16 = (bf16[22,64,128]{2,1,0:T(8,128)(2,1)S(1)}, bf16[22,64,128]{2,1,0:T(8,128)(2,1)S(1)}, u32[]{:S(2)}, u32[]{:S(2)}) collective-permute-start(bf16[22,64,128]{2,1,0:T(8,128)(2,1)S(1)} %level1_1_1.1.refs_6_.refs_3_), channel_id=1, source_target_pairs={{0,16},{1,17},{2,18},{3,19},{4,20},{5,21},{6,22},{7,23},{8,24},{9,... | collective-permute-start | bytes 1081352 | tf_op jit(solution)/shard_map/ppermute | solution.py:23
  58.8 1.4 %late_0_0.1 = (bf16[16,64,128]{2,1,0:T(8,128)(2,1)S(1)}, f32[16,64,128]{2,1,0:T(8,128)S(1)}, bf16[64,64,128]{2,1,0:T(8,128)(2,1)S(1)}) custom-call(s32[8,64]{1,0:T(8,128)S(4)} %get-tuple-element.49.refs_0_, bf16[2,64,128,128]{3,2,1,0:T(8,128)(2,1)S(1)} %get-tuple-element.51.refs_7_.refs_8_.refs_1_.refs_10_.refs_9_.refs_6_.refs_5_, ...), custom_call_target="tpu_custom_call" | custom-call | bytes 2000000 | tf_op jit(solution)/shard_map/late_0_0/pallas_call | solution.py:44
  61.1 1.6 %collective-permute-done.14.refs_2_ = bf16[21,64,128]{2,1,0:T(8,128)(2,1)S(1)} collective-permute-done((bf16[21,64,128]{2,1,0:T(8,128)(2,1)S(1)}, bf16[21,64,128]{2,1,0:T(8,128)(2,1)S(1)}, u32[]{:S(2)}, u32[]{:S(2)}) %collective-permute-start.14) | collective-permute-done | bytes 344096 | tf_op jit(solution)/shard_map/ppermute | solution.py:23
  63.3 3.1 %collective-permute-start.17 = (bf16[21,64,128]{2,1,0:T(8,128)(2,1)S(1)}, bf16[21,64,128]{2,1,0:T(8,128)(2,1)S(1)}, u32[]{:S(2)}, u32[]{:S(2)}) collective-permute-start(bf16[21,64,128]{2,1,0:T(8,128)(2,1)S(1)} %level1_1_2.1.refs_4_.refs_7_), channel_id=1, source_target_pairs={{0,16},{1,17},{2,18},{3,19},{4,20},{5,21},{6,22},{7,23},{8,24},{9,... | collective-permute-start | bytes 1032200 | tf_op jit(solution)/shard_map/ppermute | solution.py:23
  66.3 3.4 %collective-permute-start.18 = (bf16[16,64,128]{2,1,0:T(8,128)(2,1)S(1)}, bf16[16,64,128]{2,1,0:T(8,128)(2,1)S(1)}, u32[]{:S(2)}, u32[]{:S(2)}) collective-permute-start(bf16[16,64,128]{2,1,0:T(8,128)(2,1)S(1)} %get-tuple-element.74.refs_3_), channel_id=1, source_target_pairs={{0,32},{32,0},{64,96},{96,64},{1,33},{33,1},{65,97},{97,65},{2,34}... | collective-permute-start | bytes 786440 | tf_op jit(solution)/shard_map/ppermute | solution.py:23
  69.7 1.1 %early_1_0.1 = (bf16[64,64,128]{2,1,0:T(8,128)(2,1)S(1)}, bf16[43,64,128]{2,1,0:T(8,128)(2,1)S(1)}) custom-call(s32[8,64]{1,0:T(8,128)S(4)} %get-tuple-element.49.refs_0_, bf16[2,64,128,128]{3,2,1,0:T(8,128)(2,1)S(1)} %get-tuple-element.51.refs_7_.refs_8_.refs_1_.refs_10_.refs_9_.refs_6_.refs_5_, bf16[22,64,128]{2,1,0:T(8,128)(2,1)S(1)} %level1_1_0.1.refs_5_.refs_2_, ...), custom_call_target="tpu_custom_call" | custom-call | bytes 20000000 | tf_op jit(solution)/shard_map/early_1_0/pallas_call | solution.py:44
  71.0 0.9 collective-permute-start.21
  71.8 3.4 %collective-permute-done.17.refs_5_ = bf16[21,64,128]{2,1,0:T(8,128)(2,1)S(1)} collective-permute-done((bf16[21,64,128]{2,1,0:T(8,128)(2,1)S(1)}, bf16[21,64,128]{2,1,0:T(8,128)(2,1)S(1)}, u32[]{:S(2)}, u32[]{:S(2)}) %collective-permute-start.17) | collective-permute-done | bytes 344096 | tf_op jit(solution)/shard_map/ppermute | solution.py:23
  75.2 1.1 %late_1_0.1 = (bf16[16,64,128]{2,1,0:T(8,128)(2,1)S(1)}, bf16[64,64,128]{2,1,0:T(8,128)(2,1)S(1)}) custom-call(s32[8,64]{1,0:T(8,128)S(4)} %get-tuple-element.49.refs_0_, bf16[2,64,128,128]{3,2,1,0:T(8,128)(2,1)S(1)} %get-tuple-element.51.refs_7_.refs_8_.refs_1_.refs_10_.refs_9_.refs_6_.refs_5_, ...), custom_call_target="tpu_custom_call" | custom-call | bytes 2000000 | tf_op jit(solution)/shard_map/late_1_0/pallas_call | solution.py:44
  76.3 2.8 %collective-permute-start.20 = (bf16[16,64,128]{2,1,0:T(8,128)(2,1)S(1)}, bf16[16,64,128]{2,1,0:T(8,128)(2,1)S(1)}, u32[]{:S(2)}, u32[]{:S(2)}) collective-permute-start(bf16[16,64,128]{2,1,0:T(8,128)(2,1)S(1)} %get-tuple-element.81.refs_3_), channel_id=1, source_target_pairs={{0,32},{32,0},{64,96},{96,64},{1,33},{33,1},{65,97},{97,65},{2,34}... | collective-permute-start | bytes 786440 | tf_op jit(solution)/shard_map/ppermute | solution.py:23
  84.1 3.9 %collective-permute-done.22.refs_0_ = bf16[16,64,128]{2,1,0:T(8,128)(2,1)S(1)} collective-permute-done((bf16[16,64,128]{2,1,0:T(8,128)(2,1)S(1)}, bf16[16,64,128]{2,1,0:T(8,128)(2,1)S(1)}, u32[]{:S(2)}, u32[]{:S(2)}) %collective-permute-start.22) | collective-permute-done | bytes 262176 | tf_op jit(solution)/shard_map/ppermute | solution.py:23
  (44 shorter events, 14.8 us)
Async XLA Ops:
  1.6 12.6 %collective-permute-start.1 = (bf16[22,64,128]{2,1,0:T(8,128)(2,1)S(1)}, bf16[22,64,128]{2,1,0:T(8,128)(2,1)S(1)}, u32[]{:S(2)}, u32[]{:S(2)}) collective-permute-start(bf16[22,64,128]{2,1,0:T(8,128)(2,1)S(1)} %get-tuple-element.53), channel_id=1, source_target_pairs={{0,1},{1,0},{2,3},{3,2},{4,5},{5,4},{6,7},{7,6},{8,9},{9,8},{10,11... | collective-permute-start | bytes 1081352 | tf_op jit(solution)/shard_map/ppermute | solution.py:23
  8.4 13.6 %collective-permute-start = (bf16[22,64,128]{2,1,0:T(8,128)(2,1)S(1)}, bf16[22,64,128]{2,1,0:T(8,128)(2,1)S(1)}, u32[]{:S(2)}, u32[]{:S(2)}) collective-permute-start(bf16[22,64,128]{2,1,0:T(8,128)(2,1)S(1)} %get-tuple-element.52), channel_id=1, source_target_pairs={{0,1},{1,0},{2,3},{3,2},{4,5},{5,4},{6,7},{7,6},{8,9},{9,8},{10,11... | collective-permute-start | bytes 1081352 | tf_op jit(solution)/shard_map/ppermute | solution.py:23
  14.9 11.7 %collective-permute-start.5 = (bf16[22,64,128]{2,1,0:T(8,128)(2,1)S(1)}, bf16[22,64,128]{2,1,0:T(8,128)(2,1)S(1)}, u32[]{:S(2)}, u32[]{:S(2)}) collective-permute-start(bf16[22,64,128]{2,1,0:T(8,128)(2,1)S(1)} %get-tuple-element.60), channel_id=1, source_target_pairs={{0,2},{1,3},{2,0},{3,1},{4,6},{5,7},{6,4},{7,5},{8,10},{9,11},{10,... | collective-permute-start | bytes 1081352 | tf_op jit(solution)/shard_map/ppermute | solution.py:23
  16.3 13.8 %collective-permute-start.4 = (bf16[22,64,128]{2,1,0:T(8,128)(2,1)S(1)}, bf16[22,64,128]{2,1,0:T(8,128)(2,1)S(1)}, u32[]{:S(2)}, u32[]{:S(2)}) collective-permute-start(bf16[22,64,128]{2,1,0:T(8,128)(2,1)S(1)} %get-tuple-element.59), channel_id=1, source_target_pairs={{0,1},{1,0},{2,3},{3,2},{4,5},{5,4},{6,7},{7,6},{8,9},{9,8},{10,11... | collective-permute-start | bytes 1081352 | tf_op jit(solution)/shard_map/ppermute | solution.py:23
  22.7 11.7 %collective-permute-start.3 = (bf16[22,64,128]{2,1,0:T(8,128)(2,1)S(1)}, bf16[22,64,128]{2,1,0:T(8,128)(2,1)S(1)}, u32[]{:S(2)}, u32[]{:S(2)}) collective-permute-start(bf16[22,64,128]{2,1,0:T(8,128)(2,1)S(1)} %get-tuple-element.58), channel_id=1, source_target_pairs={{0,2},{1,3},{2,0},{3,1},{4,6},{5,7},{6,4},{7,5},{8,10},{9,11},{10,... | collective-permute-start | bytes 1081352 | tf_op jit(solution)/shard_map/ppermute | solution.py:23
  24.0 13.8 %collective-permute-start.2 = (bf16[22,64,128]{2,1,0:T(8,128)(2,1)S(1)}, bf16[22,64,128]{2,1,0:T(8,128)(2,1)S(1)}, u32[]{:S(2)}, u32[]{:S(2)}) collective-permute-start(bf16[22,64,128]{2,1,0:T(8,128)(2,1)S(1)} %get-tuple-element.56), channel_id=1, source_target_pairs={{0,1},{1,0},{2,3},{3,2},{4,5},{5,4},{6,7},{7,6},{8,9},{9,8},{10,11... | collective-permute-start | bytes 1081352 | tf_op jit(solution)/shard_map/ppermute | solution.py:23
  27.3 10.5 %collective-permute-start.6 = (bf16[22,64,128]{2,1,0:T(8,128)(2,1)S(1)}, bf16[22,64,128]{2,1,0:T(8,128)(2,1)S(1)}, u32[]{:S(2)}, u32[]{:S(2)}) collective-permute-start(bf16[22,64,128]{2,1,0:T(8,128)(2,1)S(1)} %level1_0_0.1.refs_5_.refs_2_), channel_id=1, source_target_pairs={{0,16},{1,17},{2,18},{3,19},{4,20},{5,21},{6,22},{7,23},{8,24},{9,... | collective-permute-start | bytes 1081352 | tf_op jit(solution)/shard_map/ppermute | solution.py:23
  30.7 11.4 %collective-permute-start.9 = (bf16[22,64,128]{2,1,0:T(8,128)(2,1)S(1)}, bf16[22,64,128]{2,1,0:T(8,128)(2,1)S(1)}, u32[]{:S(2)}, u32[]{:S(2)}) collective-permute-start(bf16[22,64,128]{2,1,0:T(8,128)(2,1)S(1)} %get-tuple-element.65), channel_id=1, source_target_pairs={{0,2},{1,3},{2,0},{3,1},{4,6},{5,7},{6,4},{7,5},{8,10},{9,11},{10,... | collective-permute-start | bytes 1081352 | tf_op jit(solution)/shard_map/ppermute | solution.py:23
  31.7 13.8 %collective-permute-start.8 = (bf16[22,64,128]{2,1,0:T(8,128)(2,1)S(1)}, bf16[22,64,128]{2,1,0:T(8,128)(2,1)S(1)}, u32[]{:S(2)}, u32[]{:S(2)}) collective-permute-start(bf16[22,64,128]{2,1,0:T(8,128)(2,1)S(1)} %get-tuple-element.64), channel_id=1, source_target_pairs={{0,1},{1,0},{2,3},{3,2},{4,5},{5,4},{6,7},{7,6},{8,9},{9,8},{10,11... | collective-permute-start | bytes 1081352 | tf_op jit(solution)/shard_map/ppermute | solution.py:23
  35.0 10.6 %collective-permute-start.10 = (bf16[22,64,128]{2,1,0:T(8,128)(2,1)S(1)}, bf16[22,64,128]{2,1,0:T(8,128)(2,1)S(1)}, u32[]{:S(2)}, u32[]{:S(2)}) collective-permute-start(bf16[22,64,128]{2,1,0:T(8,128)(2,1)S(1)} %level1_0_1.1.refs_4_.refs_3_), channel_id=1, source_target_pairs={{0,16},{1,17},{2,18},{3,19},{4,20},{5,21},{6,22},{7,23},{8,24},{9,... | collective-permute-start | bytes 1081352 | tf_op jit(solution)/shard_map/ppermute | solution.py:23
  38.5 8.4 %collective-permute-start.7 = (bf16[22,64,128]{2,1,0:T(8,128)(2,1)S(1)}, bf16[22,64,128]{2,1,0:T(8,128)(2,1)S(1)}, u32[]{:S(2)}, u32[]{:S(2)}) collective-permute-start(bf16[22,64,128]{2,1,0:T(8,128)(2,1)S(1)} %get-tuple-element.63), channel_id=1, source_target_pairs={{0,2},{1,3},{2,0},{3,1},{4,6},{5,7},{6,4},{7,5},{8,10},{9,11},{10,... | collective-permute-start | bytes 1081352 | tf_op jit(solution)/shard_map/ppermute | solution.py:23
  39.5 12.3 %collective-permute-start.12 = (bf16[20,64,128]{2,1,0:T(8,128)(2,1)S(1)}, bf16[20,64,128]{2,1,0:T(8,128)(2,1)S(1)}, u32[]{:S(2)}, u32[]{:S(2)}) collective-permute-start(bf16[20,64,128]{2,1,0:T(8,128)(2,1)S(1)} %get-tuple-element.68), channel_id=1, source_target_pairs={{0,1},{1,0},{2,3},{3,2},{4,5},{5,4},{6,7},{7,6},{8,9},{9,8},{10,11... | collective-permute-start | bytes 983048 | tf_op jit(solution)/shard_map/ppermute | solution.py:23
  42.7 11.1 %collective-permute-start.13 = (bf16[22,64,128]{2,1,0:T(8,128)(2,1)S(1)}, bf16[22,64,128]{2,1,0:T(8,128)(2,1)S(1)}, u32[]{:S(2)}, u32[]{:S(2)}) collective-permute-start(bf16[22,64,128]{2,1,0:T(8,128)(2,1)S(1)} %level1_0_2.1.refs_5_.refs_4_), channel_id=1, source_target_pairs={{0,16},{1,17},{2,18},{3,19},{4,20},{5,21},{6,22},{7,23},{8,24},{9,... | collective-permute-start | bytes 1081352 | tf_op jit(solution)/shard_map/ppermute | solution.py:23
  46.2 8.7 %collective-permute-start.11 = (bf16[22,64,128]{2,1,0:T(8,128)(2,1)S(1)}, bf16[22,64,128]{2,1,0:T(8,128)(2,1)S(1)}, u32[]{:S(2)}, u32[]{:S(2)}) collective-permute-start(bf16[22,64,128]{2,1,0:T(8,128)(2,1)S(1)} %get-tuple-element.67), channel_id=1, source_target_pairs={{0,2},{1,3},{2,0},{3,1},{4,6},{5,7},{6,4},{7,5},{8,10},{9,11},{10,... | collective-permute-start | bytes 1081352 | tf_op jit(solution)/shard_map/ppermute | solution.py:23
  47.4 12.8 %collective-permute-start.15 = (bf16[22,64,128]{2,1,0:T(8,128)(2,1)S(1)}, bf16[22,64,128]{2,1,0:T(8,128)(2,1)S(1)}, u32[]{:S(2)}, u32[]{:S(2)}) collective-permute-start(bf16[22,64,128]{2,1,0:T(8,128)(2,1)S(1)} %level1_1_0.1.refs_5_.refs_2_), channel_id=1, source_target_pairs={{0,16},{1,17},{2,18},{3,19},{4,20},{5,21},{6,22},{7,23},{8,24},{9,... | collective-permute-start | bytes 1081352 | tf_op jit(solution)/shard_map/ppermute | solution.py:23
  52.4 10.2 %collective-permute-start.14 = (bf16[21,64,128]{2,1,0:T(8,128)(2,1)S(1)}, bf16[21,64,128]{2,1,0:T(8,128)(2,1)S(1)}, u32[]{:S(2)}, u32[]{:S(2)}) collective-permute-start(bf16[21,64,128]{2,1,0:T(8,128)(2,1)S(1)} %get-tuple-element.71), channel_id=1, source_target_pairs={{0,2},{1,3},{2,0},{3,1},{4,6},{5,7},{6,4},{7,5},{8,10},{9,11},{10,... | collective-permute-start | bytes 1032200 | tf_op jit(solution)/shard_map/ppermute | solution.py:23
  55.6 14.2 %collective-permute-start.16 = (bf16[22,64,128]{2,1,0:T(8,128)(2,1)S(1)}, bf16[22,64,128]{2,1,0:T(8,128)(2,1)S(1)}, u32[]{:S(2)}, u32[]{:S(2)}) collective-permute-start(bf16[22,64,128]{2,1,0:T(8,128)(2,1)S(1)} %level1_1_1.1.refs_6_.refs_3_), channel_id=1, source_target_pairs={{0,16},{1,17},{2,18},{3,19},{4,20},{5,21},{6,22},{7,23},{8,24},{9,... | collective-permute-start | bytes 1081352 | tf_op jit(solution)/shard_map/ppermute | solution.py:23
  63.3 11.9 %collective-permute-start.17 = (bf16[21,64,128]{2,1,0:T(8,128)(2,1)S(1)}, bf16[21,64,128]{2,1,0:T(8,128)(2,1)S(1)}, u32[]{:S(2)}, u32[]{:S(2)}) collective-permute-start(bf16[21,64,128]{2,1,0:T(8,128)(2,1)S(1)} %level1_1_2.1.refs_4_.refs_7_), channel_id=1, source_target_pairs={{0,16},{1,17},{2,18},{3,19},{4,20},{5,21},{6,22},{7,23},{8,24},{9,... | collective-permute-start | bytes 1032200 | tf_op jit(solution)/shard_map/ppermute | solution.py:23
  66.3 4.6 %collective-permute-start.18 = (bf16[16,64,128]{2,1,0:T(8,128)(2,1)S(1)}, bf16[16,64,128]{2,1,0:T(8,128)(2,1)S(1)}, u32[]{:S(2)}, u32[]{:S(2)}) collective-permute-start(bf16[16,64,128]{2,1,0:T(8,128)(2,1)S(1)} %get-tuple-element.74.refs_3_), channel_id=1, source_target_pairs={{0,32},{32,0},{64,96},{96,64},{1,33},{33,1},{65,97},{97,65},{2,34}... | collective-permute-start | bytes 786440 | tf_op jit(solution)/shard_map/ppermute | solution.py:23
  69.7 2.1 %collective-permute-start.19 = (bf16[16,64,128]{2,1,0:T(8,128)(2,1)S(1)}, bf16[16,64,128]{2,1,0:T(8,128)(2,1)S(1)}, u32[]{:S(2)}, u32[]{:S(2)}) collective-permute-start(bf16[16,64,128]{2,1,0:T(8,128)(2,1)S(1)} %get-tuple-element.79), channel_id=1, source_target_pairs={{0,32},{32,0},{64,96},{96,64},{1,33},{33,1},{65,97},{97,65},{2,34}... | collective-permute-start | bytes 786440 | tf_op jit(solution)/shard_map/ppermute | solution.py:23
  71.0 8.6 %collective-permute-start.21 = (bf16[16,64,128]{2,1,0:T(8,128)(2,1)S(1)}, bf16[16,64,128]{2,1,0:T(8,128)(2,1)S(1)}, u32[]{:S(2)}, u32[]{:S(2)}) collective-permute-start(bf16[16,64,128]{2,1,0:T(8,128)(2,1)S(1)} %join_0_0.1.refs_6_), channel_id=1, source_target_pairs={{0,64},{32,96},{64,0},{96,32},{1,65},{33,97},{65,1},{97,33},{2,66}... | collective-permute-start | bytes 786440 | tf_op jit(solution)/shard_map/ppermute | solution.py:23
  76.3 4.0 %collective-permute-start.20 = (bf16[16,64,128]{2,1,0:T(8,128)(2,1)S(1)}, bf16[16,64,128]{2,1,0:T(8,128)(2,1)S(1)}, u32[]{:S(2)}, u32[]{:S(2)}) collective-permute-start(bf16[16,64,128]{2,1,0:T(8,128)(2,1)S(1)} %get-tuple-element.81.refs_3_), channel_id=1, source_target_pairs={{0,32},{32,0},{64,96},{96,64},{1,33},{33,1},{65,97},{97,65},{2,34}... | collective-permute-start | bytes 786440 | tf_op jit(solution)/shard_map/ppermute | solution.py:23
  80.3 7.6 %collective-permute-start.22 = (bf16[16,64,128]{2,1,0:T(8,128)(2,1)S(1)}, bf16[16,64,128]{2,1,0:T(8,128)(2,1)S(1)}, u32[]{:S(2)}, u32[]{:S(2)}) collective-permute-start(bf16[16,64,128]{2,1,0:T(8,128)(2,1)S(1)} %join_1_0.1.refs_3_), channel_id=1, source_target_pairs={{0,64},{32,96},{64,0},{96,32},{1,65},{33,97},{65,1},{97,33},{2,66}... | collective-permute-start | bytes 786440 | tf_op jit(solution)/shard_map/ppermute | solution.py:23
  82.0 1.7 %collective-permute-start.23 = (bf16[8,64,128]{2,1,0:T(8,128)(2,1)S(1)}, bf16[8,64,128]{2,1,0:T(8,128)(2,1)S(1)}, u32[]{:S(2)}, u32[]{:S(2)}) collective-permute-start(bf16[8,64,128]{2,1,0:T(8,128)(2,1)S(1)} %get-tuple-element.83), channel_id=1, source_target_pairs={{0,32},{32,0},{64,96},{96,64},{1,33},{33,1},{65,97},{97,65},{2,34}... | collective-permute-start | bytes 393224 | tf_op jit(solution)/shard_map/ppermute | solution.py:23
  82.7 1.3 %collective-permute-start.24 = (bf16[8,64,128]{2,1,0:T(8,128)(2,1)S(1)}, bf16[8,64,128]{2,1,0:T(8,128)(2,1)S(1)}, u32[]{:S(2)}, u32[]{:S(2)}) collective-permute-start(bf16[8,64,128]{2,1,0:T(8,128)(2,1)S(1)} %get-tuple-element.84), channel_id=1, source_target_pairs={{0,32},{32,0},{64,96},{96,64},{1,33},{33,1},{65,97},{97,65},{2,34}... | collective-permute-start | bytes 393224 | tf_op jit(solution)/shard_map/ppermute | solution.py:23
